TPU v7x, 512 devices: a whole 4x4x16 slice. The times are simulated.
512 devices in a mesh: lat: 64 (over z, y), row: 8 (over x, core).
Axes of the slice: x: 4, y: 4, z: 16, core: 2. Of those that a mesh axis runs over, the one named last changes fastest.
Arguments:
- store: bfloat16 [384, 4096], P('row'), may hold values from -6 to 6
- batch_rows: int32 [192], replicated, may hold values from 0 to 383
- bounds: int32 [5], replicated, may hold values from 1 to 64, as said below
- w_enc: bfloat16 [4096, 49152], P('row', 'lat'), may hold values from -0.09375 to 0.09375
- b_enc: float32 [49152], P('lat'), may hold values from -2.5 to -0.5
- w_dec: bfloat16 [49152, 4096], P('lat', 'row'), may hold values from -0.0546875 to 0.0546875
- b_dec: float32 [4096], P('row'), may hold values from -3 to 3
Outputs:
- grad_enc: bfloat16 [4096, 49152], P('row', 'lat')
- grad_benc: float32 [49152], P('lat')
- grad_dec: bfloat16 [49152, 4096], P('lat', 'row')
- grad_bdec: float32 [4096], P('row')
- losses: float32 [5], replicated
Inputs may be any that keep to these rules, and one draw needn't show every extreme that they name: `bounds`: strictly increasing; the last equals 64; 32 and 33 are among them.
All inputs are finite; a program needn't handle non-finite values.
Results may differ from a plain program's by a relative error of at most 0.017.
Values may be sent and summed in bfloat16 or wider, within the bound.
A program may use at most 128 MiB of HBM per device.

v0:
```python
import jax
import jax.numpy as jnp
from jax import lax
from jax.sharding import PartitionSpec as P


def prefix(shard, axis, combine, identity, reverse):
    length, index = (lax.axis_size(axis), lax.axis_index(axis))
    everything = lax.all_gather(shard.astype(jnp.bfloat16), axis)
    start = jnp.broadcast_to(jnp.asarray(identity, shard.dtype), shard.shape)

    def hop(k, before):
        at = length - 1 - k if reverse else k
        reached = at > index if reverse else at < index
        new = combine(before, everything[at].astype(shard.dtype))
        return jnp.where(reached, new, before)

    return lax.fori_loop(0, length, hop, start)


def add_terms(earlier, later):
    return earlier + later


def per_device(store, batch_rows, bounds, w_enc, b_enc, w_dec, b_dec):
    batch = batch_rows.shape[0]
    width_dev = w_enc.shape[0]
    lat_index = lax.axis_index("lat")
    columns = lax.all_to_all(store, "row", split_axis=1, concat_axis=0, tiled=True)
    batch_x = jnp.take(columns, batch_rows, axis=0)
    target = batch_x.astype(jnp.float32) - b_dec
    centred = target.astype(jnp.bfloat16)
    partial_pre = jnp.dot(centred, w_enc, preferred_element_type=jnp.float32)
    preact = lax.psum(partial_pre.astype(jnp.bfloat16), "row").astype(jnp.float32) + b_enc
    codes = jax.nn.softplus(preact).astype(jnp.bfloat16)
    part_own = jnp.dot(codes, w_dec, preferred_element_type=jnp.float32)
    lower = prefix(part_own, "lat", add_terms, jnp.zeros_like(part_own), False)
    residual_here = target - (lower + part_own)
    is_end = (bounds == lat_index + 1).astype(jnp.float32)
    ends_here = jnp.sum(is_end)
    own_error = ends_here * residual_here
    loss_parts = is_end * jnp.sum(residual_here * residual_here)
    higher = prefix(own_error, "lat", add_terms, jnp.zeros_like(own_error), True)
    suffix = higher + own_error
    part_grad = (-2.0 / batch * suffix).astype(jnp.bfloat16)
    first_dev = (lat_index == 0).astype(jnp.float32)
    bias_term = first_dev * (-2.0 / batch * jnp.sum(suffix, axis=0))
    grad_dec = lax.dot_general(
        codes, part_grad, (((0,), (0,)), ((), ())), preferred_element_type=jnp.float32
    ).astype(jnp.bfloat16)
    partial_code = lax.dot_general(
        part_grad, w_dec, (((1,), (1,)), ((), ())), preferred_element_type=jnp.float32
    )
    code_grad = lax.psum(partial_code.astype(jnp.bfloat16), "row").astype(jnp.float32)
    pre_grad = code_grad * jax.nn.sigmoid(preact)
    grad_benc = jnp.sum(pre_grad, axis=0)
    grad_enc = lax.dot_general(
        centred,
        pre_grad.astype(jnp.bfloat16),
        (((0,), (0,)), ((), ())),
        preferred_element_type=jnp.float32,
    ).astype(jnp.bfloat16)
    enc_term = jnp.dot(w_enc.astype(jnp.float32), grad_benc, precision=lax.Precision.HIGHEST)
    grad_bdec = lax.psum(bias_term - enc_term, "lat")
    losses = lax.psum(loss_parts, ("lat", "row")) / (batch * width_dev * lax.axis_size("row"))
    return (grad_enc, grad_benc, grad_dec, grad_bdec, losses)


def solution(mesh):
    return jax.shard_map(
        per_device,
        mesh=mesh,
        in_specs=(P("row", None), P(), P(), P("row", "lat"), P("lat"), P("lat", "row"), P("row")),
        out_specs=(P("row", "lat"), P("lat"), P("lat", "row"), P("row"), P()),
        check_vma=False,
    )
```

profile of v0, /device:TPU:2, one launch (start us, length us, event | category | flops | bytes accessed | tf_op | source)
XLA Modules:
  0.0 850.5 jit_solution(11345179084017616070)
XLA Ops:
  7.2 1.9 copy.15
  9.1 9.3 %all-to-all-start = ((bf16[48,8,512]{2,0,1:T(8,128)(2,1)}), bf16[48,8,512]{2,0,1:T(8,128)(2,1)S(1)}, u32[]{:S(2)}, u32[]{:S(2)}) async-start(bf16[48,8,512]{2,0,1:T(8,128)(2,1)} %bitcast.22), calls=%async_computation | async-start | bytes 786432 | tf_op jit(solution)/shard_map/all_to_all | solution.py:29
  19.8 6.1 all-to-all-done
  26.9 2.2 convolution_convert_fusion.3
  29.2 71.9 %all-reduce.3.cloned.1.call-done = bf16[192,768]{1,0:T(8,128)(2,1)} async-done(((bf16[192,768]{1,0:T(8,128)(2,1)}), bf16[192,768]{1,0:T(8,128)(2,1)}) %all-reduce.3.cloned.1.call-update) | async-done | bytes 294928 | tf_op jit(solution)/shard_map/psum | solution.py:34
  101.1 2.2 fusion.12
  103.5 1.3 fusion.7
  104.7 173.2 %all-gather.5.cloned.1.call-done = bf16[12288,512]{1,0:T(8,128)(2,1)} async-done(((bf16[192,512]{1,0:T(8,128)(2,1)}), bf16[12288,512]{1,0:T(8,128)(2,1)}) %all-gather.5.cloned.1.call-update) | async-done | bytes 12582928 | tf_op jit(solution)/shard_map/all_gather | solution.py:9
  277.9 74.0 %while.30 = (s32[]{:T(128)}, f32[192,512]{1,0:T(8,128)S(1)}, s32[]{:T(128)}, bf16[64,192,512]{2,1,0:T(8,128)(2,1)}, s32[]{:T(128)}, /*index=5*/s32[]{:T(128)}) while((s32[]{:T(128)}, f32[192,512]{1,0:T(8,128)S(1)}, s32[]{:T(128)}, bf16[64,192,512]{2,1,0:T(8,128)(2,1)}, s32[]{:T(128)}, /*index=5*/s32[]{:T(128)}) %tuple.90), condition=%wide.region_3.4_spmd.clone, body=%wide.region_2.3_spmd.clone.sunk | while | flops 393220 | bytes 983133 | solution.py:18
  279.1 1.1 add_select_fusion.4
  280.2 1.1 add_select_fusion.4
  287.2 1.1 add_select_fusion.4
  288.3 1.1 add_select_fusion.4
  289.5 1.1 add_select_fusion.4
  290.6 1.1 add_select_fusion.4
  291.8 1.1 add_select_fusion.4
  297.6 1.1 add_select_fusion.4
  298.7 1.1 add_select_fusion.4
  299.9 1.1 add_select_fusion.4
  301.0 1.1 add_select_fusion.4
  302.2 1.1 add_select_fusion.4
  309.1 1.1 add_select_fusion.4
  310.3 1.1 add_select_fusion.4
  311.5 1.1 add_select_fusion.4
  312.6 1.1 add_select_fusion.4
  313.8 1.1 add_select_fusion.4
  319.6 1.1 add_select_fusion.4
  320.7 1.1 add_select_fusion.4
  321.9 1.1 add_select_fusion.4
  323.0 1.1 add_select_fusion.4
  324.2 1.1 add_select_fusion.4
  331.1 1.1 add_select_fusion.4
  332.3 1.1 add_select_fusion.4
  333.4 1.1 add_select_fusion.4
  334.6 1.1 add_select_fusion.4
  335.7 1.1 add_select_fusion.4
  341.5 1.1 add_select_fusion.4
  342.7 1.1 add_select_fusion.4
  343.8 1.1 add_select_fusion.4
  351.9 1.5 multiply_convert_fusion.1
  353.5 166.1 %all-gather.7.cloned.1.call-done = bf16[12288,512]{1,0:T(8,128)(2,1)} async-done(((bf16[192,512]{1,0:T(8,128)(2,1)}), bf16[12288,512]{1,0:T(8,128)(2,1)}) %all-gather.7.cloned.1.call-update) | async-done | bytes 12582928 | tf_op jit(solution)/shard_map/all_gather | solution.py:9
  519.6 74.4 %while.31 = (s32[]{:T(128)}, f32[192,512]{1,0:T(8,128)S(1)}, s32[]{:T(128)}, bf16[64,192,512]{2,1,0:T(8,128)(2,1)}, s32[]{:T(128)}, /*index=5*/s32[]{:T(128)}, s32[]{:T(128)}, s32[]{:T(128)}) while((s32[]{:T(128)}, f32[192,512]{1,0:T(8,128)S(1)}, s32[]{:T(128)}, bf16[64,192,512]{2,1,0:T(8,128)(2,1)}, s32[]{:T(128)}, ...), condition=%wide.region_5.6_spmd.clone, body=%wide.region_4.5_spmd.clone.sunk | while | flops 393224 | bytes 983195 | solution.py:18
  594.0 1.4 multiply_reduce_fusion
  597.2 99.4 %psum.31 = f32[5]{0:T(128)S(1)} all-reduce(f32[5]{0:T(128)S(1)} %compare_select_fusion.2), channel_id=1, replica_groups=mesh['lat'=64,'row'=8] {'lat','row'}, use_global_device_ids=true, to_apply=%region_11.12 | all-reduce | flops 5 | bytes 40 | tf_op jit(solution)/shard_map/psum | solution.py:65
  696.6 1.5 convolution_convert_fusion
  698.6 1.2 fusion.6
  700.5 141.1 %psum.30 = f32[512]{0:T(512)} all-reduce(f32[512]{0:T(512)S(1)} %multiply_subtract_fusion), channel_id=1, replica_groups=mesh['lat'=64,'row'=8] {'lat'}, use_global_device_ids=true, to_apply=%region_9.10 | all-reduce | flops 512 | bytes 4096 | tf_op jit(solution)/shard_map/psum | solution.py:64
  841.6 2.4 convolution_convert_fusion.1
  (133 shorter events, 116.8 us)
Async XLA Ops:
  7.2 94.0 %copy-start = (bf16[768,512]{1,0:T(8,128)(2,1)S(1)}, bf16[768,512]{1,0:T(8,128)(2,1)}, u32[]{:S(2)}) copy-start(bf16[768,512]{1,0:T(8,128)(2,1)} %param.16) | copy-start | bytes 2359300
  7.2 344.8 %copy-start.5 = (f32[512]{0:T(512)S(1)}, f32[512]{0:T(512)}, u32[]{:S(2)}) copy-start(f32[512]{0:T(512)} %param.17) | copy-start | bytes 6148
  7.2 689.4 %copy-start.4 = (f32[768]{0:T(1024)S(1)}, f32[768]{0:T(1024)}, u32[]{:S(2)}) copy-start(f32[768]{0:T(1024)} %param.15) | copy-start | bytes 9220
  7.2 589.3 %copy-start.6 = (s32[5]{0:T(128)S(1)}, s32[5]{0:T(128)}, u32[]{:S(2)}) copy-start(s32[5]{0:T(128)} %param.13) | copy-start | bytes 64
  7.2 692.6 %copy-start.1 = (bf16[512,768]{1,0:T(8,128)(2,1)S(1)}, bf16[512,768]{1,0:T(8,128)(2,1)}, u32[]{:S(2)}) copy-start(bf16[512,768]{1,0:T(8,128)(2,1)} %param.14) | copy-start | bytes 2359300
  9.1 16.8 %all-to-all-start = ((bf16[48,8,512]{2,0,1:T(8,128)(2,1)}), bf16[48,8,512]{2,0,1:T(8,128)(2,1)S(1)}, u32[]{:S(2)}, u32[]{:S(2)}) async-start(bf16[48,8,512]{2,0,1:T(8,128)(2,1)} %bitcast.22), calls=%async_computation | async-start | bytes 786432 | tf_op jit(solution)/shard_map/all_to_all | solution.py:29
  18.4 82.7 %all-reduce.3.cloned.1.call-start = ((), (), s32[]{:S(2)}) async-start(), calls=%async_computation.1 | async-start | bytes 589824 | tf_op jit(solution)/shard_map/psum | solution.py:34
  29.2 248.7 %all-gather.5.cloned.1.call-start = ((), (), s32[]{:S(2)}) async-start(), calls=%async_computation.3 | async-start | bytes 12779520 | tf_op jit(solution)/shard_map/all_gather | solution.py:9
  101.1 595.4 %copy-start.2 = (bf16[192,768]{1,0:T(8,128)(2,1)S(1)}, bf16[192,768]{1,0:T(8,128)(2,1)}, u32[]{:S(2)}) copy-start(bf16[192,768]{1,0:T(8,128)(2,1)} %all-reduce.3.cloned.1.call-done) | copy-start | bytes 884740
  103.4 416.2 %all-gather.7.cloned.1.call-start = ((), (), s32[]{:S(2)}) async-start(), calls=%async_computation.4 | async-start | bytes 12779520 | tf_op jit(solution)/shard_map/all_gather | solution.py:9
  353.4 345.2 %all-reduce.5.cloned.1.call-start = ((), (), s32[]{:S(2)}) async-start(), calls=%async_computation.2 | async-start | bytes 589824 | tf_op jit(solution)/shard_map/psum | solution.py:54
  699.8 144.2 %copy-start.3 = (f32[768]{0:T(1024)}, f32[768]{0:T(1024)S(1)}, u32[]{:S(2)}) copy-start(f32[768]{0:T(1024)S(1)} %fusion.6) | copy-start | bytes 9220
Sparse Core Ops, SparseCore 0:
  29.3 71.7 all-reduce.2
  105.1 172.7 all-gather.4
  353.6 165.9 all-gather.6
  597.3 67.9 all-reduce.4
where the time goes:
time: 854 us; the launch traced here: 851 us
  waiting for transfers between devices  417 us (49%)
  blocking collectives  240 us (28%)
  other arithmetic  153 us (18%)
  between operations  13.9 us (2%)
  matrix products  10.3 us (1%)
  starting transfers between devices  9.4 us (1%)
    all_gather x2, waiting for transfers between devices, prefix(): everything = lax.all_gather(shard.astype(jnp.bfloat16), axis)  339 us
    select_n x128, other arithmetic, hop(): return jnp.where(reached, new, before)  145 us
    psum x1, blocking collectives, per_device(): grad_bdec = lax.psum(bias_term - enc_term, 'lat')  141 us
    psum x1, blocking collectives, per_device(): lax.psum(loss_parts, ('lat', 'row'))  99.4 us
    psum x1, waiting for transfers between devices, per_device(): lax.psum(partial_pre.astype(jnp.bfloat16), 'row').astype(jnp.float32)  71.9 us
  transfers between devices with their start and end apart: 5, of which 4 were waited for; matrix products, arithmetic and copies ran while one was open for 1% of the time, Pallas kernels for 0%

commit v1 on v0

v1 whole, which is shorter than its diff:
```python
import jax
import jax.numpy as jnp
from jax import lax
from jax.experimental import pallas as pl
from jax.experimental.pallas import tpu as pltpu
from jax.sharding import PartitionSpec as P

MESH = pl.DeviceIdType.MESH
BF16, F32 = jnp.bfloat16, jnp.float32

NX, NC, NY, NZ = 4, 2, 4, 16
ROWS = NX * NC
B, STORE, PREFIXES = 192, 384, 5
WIDTH, LAT = 512, 768
SB = STORE // ROWS
RB = B // NX
CB = LAT // NC
TILES = 12

X_ORDER = ((2, 0), (2, 1), (1, 0), (1, 1), (3, 0), (3, 1), (0, 1))
Z_ORDER = (8, 7, 9, 6, 10, 5, 11, 4, 12, 3, 13, 2, 14, 1, 15)
T_ORDER = (6, 5, 7, 4, 8, 3, 9, 2, 10, 1, 11, 0)

L_ENC, L_DEC, L_STORE, L_GDEC, L_GENC = range(5)
(S_STORE, S_PRE, S_CODES, S_PART, S_ZOUT, S_RET, S_GRAD, S_CODE, S_PG, S_SUM, S_LOSS, S_BY, S_BZ) = range(13)


def owner_z(t):
    return (t // 3) * 4 + lax.rem(t, 3)


def kernel(
    store, batch_rows, bounds, w_enc, b_enc, w_dec, b_dec,
    grad_enc, grad_benc, grad_dec, tail,
    wenc, wdec, cols, target, centred, pre_out, pre_in, sig, codes, part_out, ybuf, zout, zin, rout, rin,
    gout, pgrad, code_out, code_in, pgb, sums, lbuf, gdec, genc, by, bz,
    local_sem, send_sem, recv_sem, codes_sem, grad_sem,
):
    lat, row = lax.axis_index("lat"), lax.axis_index("row")
    z, y = lat // NY, lax.rem(lat, NY)
    x, c = row // NC, lax.rem(row, NC)

    def row_peers():
        for dx, dc in X_ORDER:
            yield lax.rem(x + dx, NX), lax.rem(c + dc, NC)

    def send(src, dst, sem, recv, lat_to, row_to):
        pltpu.make_async_remote_copy(
            src_ref=src, dst_ref=dst, send_sem=send_sem.at[sem], recv_sem=recv,
            device_id=(lat_to, row_to), device_id_type=MESH,
        ).start()

    def wait(ref, sem):
        pltpu.make_async_copy(ref, ref, sem).wait()

    def block(ref, xx, cc):
        return ref.at[pl.ds(pl.multiple_of(xx * RB, RB), RB), pl.ds(pl.multiple_of(cc * CB, CB), CB)]

    def band(ref, i):
        return ref.at[pl.ds(pl.multiple_of(i * RB, RB), RB)]

    get_enc = pltpu.make_async_copy(w_enc, wenc, local_sem.at[L_ENC])
    get_dec = pltpu.make_async_copy(w_dec, wdec, local_sem.at[L_DEC])
    own_cols = pl.ds(pl.multiple_of(row * WIDTH, WIDTH), WIDTH)
    own_slot = pl.ds(pl.multiple_of(row * SB, SB), SB)
    get_own = pltpu.make_async_copy(store.at[:, own_cols], cols.at[own_slot], local_sem.at[L_STORE])
    get_own.start()
    get_enc.start()
    get_dec.start()

    barrier = pltpu.get_barrier_semaphore()
    for xx, cc in row_peers():
        pl.semaphore_signal(barrier, inc=1, device_id=(lat, xx * NC + cc), device_id_type=MESH)
    for d in range(1, NY):
        pl.semaphore_signal(barrier, inc=1, device_id=(z * NY + lax.rem(y + d, NY), row), device_id_type=MESH)
    for d in Z_ORDER:
        pl.semaphore_signal(barrier, inc=1, device_id=(lax.rem(z + d, NZ) * NY + y, row), device_id_type=MESH)
    pl.semaphore_wait(barrier, ROWS - 1 + NY - 1 + NZ - 1)

    for xx, cc in row_peers():
        to = xx * NC + cc
        their_cols = pl.ds(pl.multiple_of(to * WIDTH, WIDTH), WIDTH)
        send(store.at[:, their_cols], cols.at[own_slot], S_STORE, recv_sem.at[S_STORE], lat, to)
    get_own.wait()
    wait(cols.at[pl.ds(0, SB * (ROWS - 1))], recv_sem.at[S_STORE])
    picks = (lax.broadcasted_iota(jnp.int32, (STORE, B), 0) == batch_rows[...]).astype(BF16)
    batch_x = lax.dot_general(picks, cols[...], (((0,), (0,)), ((), ())), preferred_element_type=F32)
    target[...] = batch_x - b_dec[...]
    centred[...] = target[...].astype(BF16)

    get_enc.wait()
    pre_out[...] = jnp.dot(centred[...], wenc[...], preferred_element_type=F32).astype(BF16)
    for xx, cc in row_peers():
        send(block(pre_out, xx, cc), pre_in.at[row], S_PRE, recv_sem.at[S_PRE], lat, xx * NC + cc)
    pre_in[row] = block(pre_out, x, c)[...]
    wait(pre_in.at[pl.ds(0, ROWS - 1)], recv_sem.at[S_PRE])
    preact = b_enc[:, pl.ds(pl.multiple_of(c * CB, CB), CB)] + pre_in[0].astype(F32)
    for r in range(1, ROWS):
        preact = preact + pre_in[r].astype(F32)
    small = jnp.exp(-jnp.abs(preact))
    log1p = jnp.where(small < 1e-3, small * (1.0 - 0.5 * small), jnp.log(1.0 + small))
    block(codes, x, c)[...] = (jnp.maximum(preact, 0.0) + log1p).astype(BF16)
    for xx, cc in row_peers():
        send(block(codes, x, c), block(codes, x, c), S_CODES, codes_sem.at[x], lat, xx * NC + cc)
    sig[...] = jnp.where(preact >= 0.0, 1.0, small) / (1.0 + small)

    get_dec.wait()
    for d in (0, 1, 3, 2):
        xx = lax.rem(x + d, NX)
        if d == 0:
            wait(block(codes, xx, 0), codes_sem.at[xx])
        else:
            wait(band(codes, xx), codes_sem.at[xx])
        part = jnp.dot(band(codes, xx)[...], wdec[...], preferred_element_type=F32).astype(BF16)
        band(part_out, xx)[...] = part

        @pl.when(xx != y)
        def _():
            send(band(part_out, xx), ybuf.at[y], S_PART, recv_sem.at[S_PART], z * NY + xx, row)

    ybuf[y] = band(part_out, y)[...]
    wait(ybuf.at[pl.ds(0, NY - 1)], recv_sem.at[S_PART])

    ends = [
        [jnp.where(bounds[k] == z * NY + j + 1, 1.0, 0.0).astype(F32) for k in range(PREFIXES)] for j in range(NY)
    ]
    ends_at = [sum(ends[j][1:], ends[j][0]) for j in range(NY)]
    total = ybuf[0].astype(F32)
    cut = ends_at[0] * total
    for j in range(1, NY):
        total = total + ybuf[j].astype(F32)
        cut = cut + ends_at[j] * total
    for t in range(TILES):
        i, k = divmod(t, 4)
        zout[t, 0] = total[16 * i : 16 * i + 16, 128 * k : 128 * k + 128].astype(BF16)
        zout[t, 1] = cut[16 * i : 16 * i + 16, 128 * k : 128 * k + 128].astype(BF16)
    is_owner = lax.rem(z, 4) < 3
    own_t = (z // 4) * 3 + jnp.minimum(lax.rem(z, 4), 2)
    for d in T_ORDER:
        t = lax.rem(own_t + d, TILES)
        to = owner_z(t)

        @pl.when(to != z)
        def _():
            send(zout.at[t], zin.at[z], S_ZOUT, recv_sem.at[S_ZOUT], to * NY + y, row)

    @pl.when(is_owner)
    def _():
        zin[z] = zout[own_t]
        rows = pl.ds(pl.multiple_of(y * RB + 16 * (own_t // 4), 16), 16)
        columns = pl.ds(pl.multiple_of(128 * lax.rem(own_t, 4), 128), 128)
        goal = target[rows, columns]
        wait(zin.at[pl.ds(0, NZ - 1)], recv_sem.at[S_ZOUT])
        below = jnp.zeros((16, 128), F32)
        errors = []
        for p in range(NZ):
            rout[p, 0] = below.astype(BF16)
            number = jnp.float32(0.0)
            for k in range(PREFIXES):
                inside = jnp.logical_and(bounds[k] > p * NY, bounds[k] <= (p + 1) * NY)
                number = number + jnp.where(inside, 1.0, 0.0).astype(F32)
            errors.append(number * (goal - below) - zin[p, 1].astype(F32))
            below = below + zin[p, 0].astype(F32)
        above = jnp.zeros((16, 128), F32)
        for p in range(NZ - 1, -1, -1):
            rout[p, 1] = above.astype(BF16)
            above = above + errors[p]
        for d in Z_ORDER:
            to = lax.rem(z + d, NZ)
            send(rout.at[to], rin.at[own_t], S_RET, recv_sem.at[S_RET], to * NY + y, row)
        rin[own_t] = rout[z]
        wait(rin.at[pl.ds(0, TILES - 1)], recv_sem.at[S_RET])

    @pl.when(jnp.logical_not(is_owner))
    def _():
        wait(rin, recv_sem.at[S_RET])

    def assemble(which):
        bands = [jnp.concatenate([rin[4 * i + k, which] for k in range(4)], axis=1) for i in range(3)]
        return jnp.concatenate(bands, axis=0).astype(F32)

    goal = band(target, y)[...] - assemble(0)
    suffix = assemble(1)
    inclusive = []
    running = ybuf[0].astype(F32)
    for j in range(NY):
        if j:
            running = running + ybuf[j].astype(F32)
        inclusive.append(goal - running)
    for j in range(NY - 1, -1, -1):
        suffix = suffix + ends_at[j] * inclusive[j]
        gout[j] = (-2.0 / B * suffix).astype(BF16)

        @pl.when(j != y)
        def _():
            send(gout.at[j], band(pgrad, y), S_GRAD, grad_sem.at[y], z * NY + j, row)

    band(pgrad, y)[...] = gout[y]

    for d in (0, 1, 3, 2):
        yy = lax.rem(y + d, NY)
        if d:
            wait(band(pgrad, yy), grad_sem.at[yy])
        partial = lax.dot_general(
            band(pgrad, yy)[...], wdec[...], (((1,), (1,)), ((), ())), preferred_element_type=F32
        )
        band(code_out, yy)[...] = partial.astype(BF16)
        for dc in range(NC):
            cc = lax.rem(c + dc, NC)
            to = yy * NC + cc

            @pl.when(to != row)
            def _():
                send(block(code_out, yy, cc), code_in.at[row], S_CODE, recv_sem.at[S_CODE], lat, to)

    code_in[row] = block(code_out, x, c)[...]

    lane = lax.broadcasted_iota(jnp.int32, (1, 128), 1)
    loss_row = jnp.zeros((1, 128), F32)
    ended = jnp.zeros((RB, WIDTH), F32)
    for j in range(NY):
        square = jnp.sum(inclusive[j] * inclusive[j], axis=0, keepdims=True)
        square = jnp.sum(square, axis=1, keepdims=True)
        mark = jnp.zeros((1, 128), F32)
        for k in range(PREFIXES):
            mark = mark + jnp.where(lane == k, ends[j][k], 0.0)
        loss_row = loss_row + square * mark
        ended = ended + ends_at[j] * inclusive[j]
    bias_row = -2.0 / B * jnp.sum(ended, axis=0, keepdims=True)
    lbuf[row] = jnp.broadcast_to(loss_row, (8, 128))
    for xx, cc in row_peers():
        send(lbuf.at[row], lbuf.at[row], S_LOSS, recv_sem.at[S_LOSS], lat, xx * NC + cc)

    gdec[...] = lax.dot_general(
        codes[...], pgrad[...], (((0,), (0,)), ((), ())), preferred_element_type=F32
    ).astype(BF16)
    put_dec = pltpu.make_async_copy(gdec, grad_dec, local_sem.at[L_GDEC])
    put_dec.start()

    wait(code_in.at[pl.ds(0, ROWS - 1)], recv_sem.at[S_CODE])
    code_grad = code_in[0].astype(F32)
    for r in range(1, ROWS):
        code_grad = code_grad + code_in[r].astype(F32)
    pre_grad = code_grad * sig[...]
    row_sum = pre_grad[0:8]
    for i in range(1, RB // 8):
        row_sum = row_sum + pre_grad[8 * i : 8 * i + 8]
    sums[row] = row_sum
    block(pgb, x, c)[...] = pre_grad.astype(BF16)
    for xx, cc in row_peers():
        send(sums.at[row], sums.at[row], S_SUM, recv_sem.at[S_SUM], lat, xx * NC + cc)
    for xx, cc in row_peers():
        send(block(pgb, x, c), block(pgb, x, c), S_PG, recv_sem.at[S_PG], lat, xx * NC + cc)

    wait(sums.at[pl.ds(0, ROWS - 1)], recv_sem.at[S_SUM])
    halves = []
    for cc in range(NC):
        half = sums[cc]
        for xx in range(1, NX):
            half = half + sums[xx * NC + cc]
        halves.append(jnp.sum(half, axis=0, keepdims=True))
    benc = jnp.concatenate(halves, axis=1)
    grad_benc[...] = benc
    high = benc.astype(BF16)
    middle = (benc - high.astype(F32)).astype(BF16)
    low = (benc - high.astype(F32) - middle.astype(F32)).astype(BF16)
    three = jnp.concatenate([high, middle, low, jnp.zeros((13, LAT), BF16)], axis=0)
    term = lax.dot_general(three, wenc[...], (((1,), (1,)), ((), ())), preferred_element_type=F32)
    bias_row = bias_row - (term[0:1] + (term[1:2] + term[2:3]))
    wait(lbuf.at[pl.ds(0, ROWS - 1)], recv_sem.at[S_LOSS])
    loss_all = lbuf[0, 0:1]
    for r in range(1, ROWS):
        loss_all = loss_all + lbuf[r, 0:1]
    pieces = [bias_row[:, 128 * k : 128 * k + 128] for k in range(4)]
    by[y] = jnp.concatenate(pieces + [loss_all, jnp.zeros((3, 128), F32)], axis=0)
    for d in range(1, NY):
        send(by.at[y], by.at[y], S_BY, recv_sem.at[S_BY], z * NY + lax.rem(y + d, NY), row)

    wait(code_in.at[pl.ds(0, ROWS - 1)], recv_sem.at[S_PG])
    genc[...] = lax.dot_general(
        centred[...], pgb[...], (((0,), (0,)), ((), ())), preferred_element_type=F32
    ).astype(BF16)
    put_enc = pltpu.make_async_copy(genc, grad_enc, local_sem.at[L_GENC])
    put_enc.start()

    wait(by.at[pl.ds(0, NY - 1)], recv_sem.at[S_BY])
    bz[z] = (by[0] + by[1]) + (by[2] + by[3])
    for d in Z_ORDER:
        to = lax.rem(z + d, NZ)
        send(bz.at[z], bz.at[z], S_BZ, recv_sem.at[S_BZ], to * NY + y, row)
    wait(bz.at[pl.ds(0, NZ - 1)], recv_sem.at[S_BZ])
    everything = bz[0]
    for p in range(1, NZ):
        everything = everything + bz[p]
    tail[...] = everything

    wait(cols.at[pl.ds(0, SB * (ROWS - 1))], send_sem.at[S_STORE])
    wait(pre_in.at[pl.ds(0, ROWS - 1)], send_sem.at[S_PRE])
    wait(pre_in.at[pl.ds(0, ROWS - 1)], send_sem.at[S_CODES])
    wait(ybuf.at[pl.ds(0, NY - 1)], send_sem.at[S_PART])

    @pl.when(is_owner)
    def _():
        wait(zout.at[pl.ds(0, TILES - 1)], send_sem.at[S_ZOUT])
        wait(rout.at[pl.ds(0, NZ - 1)], send_sem.at[S_RET])

    @pl.when(jnp.logical_not(is_owner))
    def _():
        wait(zout, send_sem.at[S_ZOUT])

    wait(gout.at[pl.ds(0, NY - 1)], send_sem.at[S_GRAD])
    wait(code_in.at[pl.ds(0, ROWS - 1)], send_sem.at[S_CODE])
    wait(code_in.at[pl.ds(0, ROWS - 1)], send_sem.at[S_PG])
    wait(sums.at[pl.ds(0, ROWS - 1)], send_sem.at[S_SUM])
    wait(lbuf.at[pl.ds(0, ROWS - 1)], send_sem.at[S_LOSS])
    wait(by.at[pl.ds(0, NY - 1)], send_sem.at[S_BY])
    wait(bz.at[pl.ds(0, NZ - 1)], send_sem.at[S_BZ])
    put_dec.wait()
    put_enc.wait()


def per_device(store, batch_rows, bounds, w_enc, b_enc, w_dec, b_dec):
    vmem, hbm = pl.BlockSpec(memory_space=pltpu.VMEM), pl.BlockSpec(memory_space=pl.ANY)
    smem = pl.BlockSpec(memory_space=pltpu.SMEM)
    grad_enc, grad_benc, grad_dec, tail = pl.pallas_call(
        kernel,
        out_shape=(
            jax.ShapeDtypeStruct((WIDTH, LAT), BF16),
            jax.ShapeDtypeStruct((1, LAT), F32),
            jax.ShapeDtypeStruct((LAT, WIDTH), BF16),
            jax.ShapeDtypeStruct((8, 128), F32),
        ),
        in_specs=[hbm, vmem, smem, hbm, vmem, hbm, vmem],
        out_specs=(hbm, vmem, hbm, vmem),
        scratch_shapes=[
            pltpu.VMEM((WIDTH, LAT), BF16),
            pltpu.VMEM((LAT, WIDTH), BF16),
            pltpu.VMEM((STORE, WIDTH), BF16),
            pltpu.VMEM((B, WIDTH), F32),
            pltpu.VMEM((B, WIDTH), BF16),
            pltpu.VMEM((B, LAT), BF16),
            pltpu.VMEM((ROWS, RB, CB), BF16),
            pltpu.VMEM((RB, CB), F32),
            pltpu.VMEM((B, LAT), BF16),
            pltpu.VMEM((B, WIDTH), BF16),
            pltpu.VMEM((NY, RB, WIDTH), BF16),
            pltpu.VMEM((TILES, 2, 16, 128), BF16),
            pltpu.VMEM((NZ, 2, 16, 128), BF16),
            pltpu.VMEM((NZ, 2, 16, 128), BF16),
            pltpu.VMEM((TILES, 2, 16, 128), BF16),
            pltpu.VMEM((NY, RB, WIDTH), BF16),
            pltpu.VMEM((B, WIDTH), BF16),
            pltpu.VMEM((B, LAT), BF16),
            pltpu.VMEM((ROWS, RB, CB), BF16),
            pltpu.VMEM((B, LAT), BF16),
            pltpu.VMEM((ROWS, 8, CB), F32),
            pltpu.VMEM((ROWS, 8, 128), F32),
            pltpu.VMEM((LAT, WIDTH), BF16),
            pltpu.VMEM((WIDTH, LAT), BF16),
            pltpu.VMEM((NY, 8, 128), F32),
            pltpu.VMEM((NZ, 8, 128), F32),
            pltpu.SemaphoreType.DMA((5,)),
            pltpu.SemaphoreType.DMA((13,)),
            pltpu.SemaphoreType.DMA((13,)),
            pltpu.SemaphoreType.DMA((NX,)),
            pltpu.SemaphoreType.DMA((NY,)),
        ],
        compiler_params=pltpu.CompilerParams(
            collective_id=0, has_side_effects=True, vmem_limit_bytes=40 * 2**20
        ),
        name="sae_step",
    )(store, batch_rows.reshape(1, B), bounds, w_enc, b_enc.reshape(1, LAT), w_dec, b_dec.reshape(1, WIDTH))
    return (
        grad_enc,
        grad_benc.reshape(LAT),
        grad_dec,
        tail[:4].reshape(WIDTH),
        tail[4, :PREFIXES] * (1.0 / (B * WIDTH * ROWS)),
    )


def solution(mesh):
    return jax.shard_map(
        per_device,
        mesh=mesh,
        in_specs=(P("row", None), P(), P(), P("row", "lat"), P("lat"), P("lat", "row"), P("row")),
        out_specs=(P("row", "lat"), P("lat"), P("lat", "row"), P("row"), P()),
        check_vma=False,
    )
```

time: 854 us -> 89 us (0.10)
  the two profiles are of different devices: /device:TPU:2 before, /device:TPU:1 now
where the time goes in v1:
time: 89 us; the launch traced here: 88.6 us
  Pallas kernels  79.8 us (90%)
  local copies, waits for them, and re-layouts  6.98 us (8%)
  other arithmetic  1.12 us (1%)
    pallas_call x1, Pallas kernels, per_device(): pl.pallas_call(kernel, out_shape=(jax.ShapeDtypeStruct((WIDTH, LAT), BF16...  79.8 us
    unnamed x14, local copies, waits for them, and re-layouts  5.71 us

profile of v1, /device:TPU:1, one launch (start us, length us, event | category | flops | bytes accessed | tf_op | source)
XLA Modules:
  0.0 88.6 jit_solution(6101323856370970485)
XLA Ops:
  0.6 0.7 reshape.28.b_enc
  1.3 0.0 copy-start.3
  1.3 0.0 copy-start.4
  1.3 0.0 copy-start.5
  1.3 0.7 copy-done.3
  2.0 0.0 copy-done.4
  2.0 0.0 copy-done.5
  2.0 0.0 copy-start
  2.0 1.1 %copy-done = bf16[512,768]{1,0:T(8,128)(2,1)S(1)} copy-done((bf16[512,768]{1,0:T(8,128)(2,1)S(1)}, bf16[512,768]{1,0:T(8,128)(2,1)}, u32[]{:S(2)}) %copy-start) | copy-done | bytes 786456
  3.2 0.0 copy-start.1
  3.2 1.1 %copy-done.1 = bf16[768,512]{1,0:T(8,128)(2,1)S(1)} copy-done((bf16[768,512]{1,0:T(8,128)(2,1)S(1)}, bf16[768,512]{1,0:T(8,128)(2,1)}, u32[]{:S(2)}) %copy-start.1) | copy-done | bytes 786456
  4.3 0.0 copy-start.2
  4.3 1.0 %copy-done.2 = bf16[48,4096]{1,0:T(8,128)(2,1)S(1)} copy-done((bf16[48,4096]{1,0:T(8,128)(2,1)S(1)}, bf16[48,4096]{1,0:T(8,128)(2,1)}, u32[]{:S(2)}) %copy-start.2) | copy-done | bytes 393240
  5.3 79.8 %sae_step.1 = (bf16[512,768]{1,0:T(8,128)(2,1)S(1)}, f32[1,768]{1,0:T(1,128)S(1)}, bf16[768,512]{1,0:T(8,128)(2,1)S(1)}, f32[8,128]{1,0:T(8,128)S(1)}) custom-call(bf16[48,4096]{1,0:T(8,128)(2,1)S(1)} %copy-done.2, s32[1,192]{1,0:T(1,128)S(1)} %bitcast.7, s32[5]{0:T(128)S(1)} %copy-done.5, bf16[512,768]{1,0:T(8,128)(2,1)S(1)} %copy-done, ...), custom_call_target="tpu_custom_call" | custom-call | tf_op jit(solution)/shard_map/sae_step/pallas_call | solution.py:325
  85.1 0.6 slice_bitcast_fusion
  85.7 0.5 multiply_bitcast_fusion
  86.2 0.6 reduce
  86.8 0.9 copy.14
  87.7 0.9 copy.15
Async XLA Ops:
  1.3 0.7 copy-start.3
  1.3 0.7 copy-start.4
  1.3 0.7 copy-start.5
  2.0 1.1 %copy-start = (bf16[512,768]{1,0:T(8,128)(2,1)S(1)}, bf16[512,768]{1,0:T(8,128)(2,1)}, u32[]{:S(2)}) copy-start(bf16[512,768]{1,0:T(8,128)(2,1)} %w_enc.1) | copy-start | bytes 2359300
  3.2 1.1 %copy-start.1 = (bf16[768,512]{1,0:T(8,128)(2,1)S(1)}, bf16[768,512]{1,0:T(8,128)(2,1)}, u32[]{:S(2)}) copy-start(bf16[768,512]{1,0:T(8,128)(2,1)} %w_dec.1) | copy-start | bytes 2359300
  4.3 1.0 %copy-start.2 = (bf16[48,4096]{1,0:T(8,128)(2,1)S(1)}, bf16[48,4096]{1,0:T(8,128)(2,1)}, u32[]{:S(2)}) copy-start(bf16[48,4096]{1,0:T(8,128)(2,1)} %store.1) | copy-start | bytes 1179652

commit v2 on v1

v2 whole, which is shorter than its diff:
```python
import jax
import jax.numpy as jnp
from jax import lax
from jax.experimental import pallas as pl
from jax.experimental.pallas import tpu as pltpu
from jax.sharding import PartitionSpec as P

MESH = pl.DeviceIdType.MESH
BF16, F32 = jnp.bfloat16, jnp.float32

NX, NC, NY, NZ = 4, 2, 4, 16
ROWS = NX * NC
B, STORE, PREFIXES = 192, 384, 5
WIDTH, LAT = 512, 768
SB = STORE // ROWS
GROUPS = 3
GR = B // GROUPS
RT = GR // NX
CB = LAT // NC
TILES = WIDTH // 128

X_ORDER = ((2, 0), (2, 1), (1, 0), (1, 1), (3, 0), (3, 1), (0, 1))
Z_ORDER = (8, 7, 9, 6, 10, 5, 11, 4, 12, 3, 13, 2, 14, 1, 15)
Y_ORDER = (2, 1, 3)

L_ENC, L_DEC, L_STORE, L_GDEC, L_GENC, L_ROWS, L_BENC, L_BDEC, L_BOUNDS = range(9)
S_PRE, S_CODES, S_PART, S_RET, S_GRAD, S_CODE = range(0, 18, 3)
S_STORE, S_ZOUT, S_PG, S_SUM, S_LOSS, S_BY, S_BZ = range(18, 25)


def kernel(
    store, batch_rows_hbm, bounds_hbm, w_enc, b_enc_hbm, w_dec, b_dec_hbm,
    grad_enc, grad_benc, grad_dec, tail,
    batch_rows, bounds, b_enc_flat, b_enc, b_dec, wenc, wdec, wenc_t, wdec_t, picks, cols, target, centred, pre_out, pre_in, sig, codes, part_out, ybuf, zout, zin, rout, rin,
    gout, pgrad, code_out, code_in, pgb, sums, lbuf, gdec, genc, by, bz,
    local_sem, send_sem, recv_sem, relay_sem,
):
    lat, row = lax.axis_index("lat"), lax.axis_index("row")
    z, y = lat // NY, lax.rem(lat, NY)
    x, c = row // NC, lax.rem(row, NC)

    def row_peers():
        for dx, dc in X_ORDER:
            yield lax.rem(x + dx, NX), lax.rem(c + dc, NC)

    def send(src, dst, sem, recv, lat_to, row_to):
        pltpu.make_async_remote_copy(
            src_ref=src, dst_ref=dst, send_sem=send_sem.at[sem], recv_sem=recv,
            device_id=(lat_to, row_to), device_id_type=MESH,
        ).start()

    def wait(ref, sem):
        pltpu.make_async_copy(ref, ref, sem).wait()

    def group(g):
        return pl.ds(g * GR, GR)

    def band(ref, g, i):
        return ref.at[pl.ds(pl.multiple_of(g * GR + i * RT, RT), RT)]

    def block(ref, g, xx, cc):
        return band(ref, g, xx).at[:, pl.ds(pl.multiple_of(cc * CB, CB), CB)]

    get_enc = pltpu.make_async_copy(w_enc, wenc, local_sem.at[L_ENC])
    get_dec = pltpu.make_async_copy(w_dec, wdec, local_sem.at[L_DEC])
    own_cols = pl.ds(pl.multiple_of(row * WIDTH, WIDTH), WIDTH)
    own_slot = pl.ds(pl.multiple_of(row * SB, SB), SB)
    get_own = pltpu.make_async_copy(store.at[:, own_cols], cols.at[own_slot], local_sem.at[L_STORE])
    get_rows = pltpu.make_async_copy(batch_rows_hbm, batch_rows, local_sem.at[L_ROWS])
    get_benc = pltpu.make_async_copy(b_enc_hbm, b_enc_flat, local_sem.at[L_BENC])
    get_bdec = pltpu.make_async_copy(b_dec_hbm, b_dec, local_sem.at[L_BDEC])
    get_bounds = pltpu.make_async_copy(bounds_hbm, bounds, local_sem.at[L_BOUNDS])
    gets = (get_own, get_rows, get_bdec, get_enc, get_benc, get_dec, get_bounds)
    for get in gets:
        get.start()
    pending = []

    barrier = pltpu.get_barrier_semaphore()
    for xx, cc in row_peers():
        pl.semaphore_signal(barrier, inc=1, device_id=(lat, xx * NC + cc), device_id_type=MESH)
    for d in range(1, NY):
        pl.semaphore_signal(barrier, inc=1, device_id=(z * NY + lax.rem(y + d, NY), row), device_id_type=MESH)
    next_z, last_z = lax.rem(z + 1, NZ) * NY + y, lax.rem(z + NZ - 1, NZ) * NY + y
    for to in (next_z, last_z):
        pl.semaphore_signal(barrier, inc=1, device_id=(to, row), device_id_type=MESH)
    pl.semaphore_wait(barrier, ROWS - 1 + NY - 1 + 2)

    def pass_on():
        pl.semaphore_signal(relay_sem.at[0], inc=1, device_id=(next_z, row), device_id_type=MESH)
        pl.semaphore_signal(relay_sem.at[1], inc=1, device_id=(last_z, row), device_id_type=MESH)

    def relay(last=False):
        pl.semaphore_wait(relay_sem.at[0], 1)
        pl.semaphore_wait(relay_sem.at[1], 1)
        if not last:
            pass_on()

    pass_on()

    for xx, cc in row_peers():
        to = xx * NC + cc
        their_cols = pl.ds(pl.multiple_of(to * WIDTH, WIDTH), WIDTH)
        send(store.at[:, their_cols], cols.at[own_slot], S_STORE, recv_sem.at[S_STORE], lat, to)
    pending.append((cols.at[pl.ds(0, SB * (ROWS - 1))], S_STORE))
    for get in gets:
        get.wait()
    b_enc[...] = b_enc_flat[...].reshape(1, LAT)
    rows_down = jnp.broadcast_to(batch_rows[...], (128, B)).T
    lanes = lax.broadcasted_iota(jnp.int32, (B, 128), 1)
    for k in range(STORE // 128):
        picks[:, 128 * k : 128 * k + 128] = (lanes + 128 * k == rows_down).astype(BF16)
    relay()
    relay()
    relay()
    wait(cols.at[pl.ds(0, SB * (ROWS - 1))], recv_sem.at[S_STORE])
    for g in range(GROUPS):
        rows = group(g)
        goal = jnp.dot(picks[rows], cols[...], preferred_element_type=F32) - b_dec[...]
        target[rows] = goal
        centred[rows] = goal.astype(BF16)
        pre_out[rows] = jnp.dot(centred[rows], wenc[...], preferred_element_type=F32).astype(BF16)
        for xx, cc in row_peers():
            send(block(pre_out, g, xx, cc), pre_in.at[g, row], S_PRE, recv_sem.at[S_PRE + g], lat, xx * NC + cc)
    pending.append((pre_in.at[:, pl.ds(0, ROWS - 1)], S_PRE))
    relay()
    relay()
    wenc_t[...] = wenc[...].T
    my_b_enc = b_enc[:, pl.ds(pl.multiple_of(c * CB, CB), CB)]
    for g in range(GROUPS):
        pre_in[g, row] = block(pre_out, g, x, c)[...]
        wait(pre_in.at[g, pl.ds(0, ROWS - 1)], recv_sem.at[S_PRE + g])
        preact = my_b_enc + pre_in[g, 0].astype(F32)
        for r in range(1, ROWS):
            preact = preact + pre_in[g, r].astype(F32)
        small = jnp.exp(-jnp.abs(preact))
        log1p = jnp.where(small < 1e-3, small * (1.0 - 0.5 * small), jnp.log(1.0 + small))
        block(codes, g, x, c)[...] = (jnp.maximum(preact, 0.0) + log1p).astype(BF16)
        for xx, cc in row_peers():
            send(block(codes, g, x, c), block(codes, g, x, c), S_CODES, recv_sem.at[S_CODES + g], lat, xx * NC + cc)
        sig[g] = jnp.where(preact >= 0.0, 1.0, small) / (1.0 + small)
    pending.append((pre_in.at[:, pl.ds(0, ROWS - 1)], S_CODES))

    relay()
    relay(last=True)
    wdec_t[...] = wdec[...].T
    for g in range(GROUPS):
        wait(pre_in.at[g, pl.ds(0, ROWS - 1)], recv_sem.at[S_CODES + g])
        part_out[group(g)] = jnp.dot(codes[group(g)], wdec[...], preferred_element_type=F32).astype(BF16)
        for d in Y_ORDER:
            to = lax.rem(y + d, NY)
            send(band(part_out, g, to), ybuf.at[g, y], S_PART, recv_sem.at[S_PART + g], z * NY + to, row)
        ybuf[g, y] = band(part_out, g, y)[...]
    pending.append((ybuf.at[:, pl.ds(0, NY - 1)], S_PART))

    ends = [
        [jnp.where(bounds[k] == z * NY + j + 1, 1.0, 0.0).astype(F32) for k in range(PREFIXES)] for j in range(NY)
    ]
    ends_at = [sum(ends[j][1:], ends[j][0]) for j in range(NY)]
    number = []
    for p in range(NZ):
        inside = [jnp.logical_and(bounds[k] > p * NY, bounds[k] <= (p + 1) * NY) for k in range(PREFIXES)]
        counts = [jnp.where(one, 1.0, 0.0).astype(F32) for one in inside]
        number.append(sum(counts[1:], counts[0]))
    for g in range(GROUPS):
        wait(ybuf.at[g, pl.ds(0, NY - 1)], recv_sem.at[S_PART + g])
        total = ybuf[g, 0].astype(F32)
        cut = ends_at[0] * total
        for j in range(1, NY):
            total = total + ybuf[g, j].astype(F32)
            cut = cut + ends_at[j] * total
        for k in range(TILES):
            zout[g, k, 0] = total[:, 128 * k : 128 * k + 128].astype(BF16)
            zout[g, k, 1] = cut[:, 128 * k : 128 * k + 128].astype(BF16)
        for d in range(TILES):
            k = lax.rem(z // 4 + (2, 1, 3, 0)[d], TILES)
            to = 4 * k + g

            @pl.when(to != z)
            def _():
                send(zout.at[g, k], zin.at[z], S_ZOUT, recv_sem.at[S_ZOUT], to * NY + y, row)

    own_g, own_k = lax.rem(z, 4), z // 4
    is_owner = own_g < GROUPS

    @pl.when(is_owner)
    def _():
        zin[z] = zout[own_g, own_k]
        rows = pl.ds(pl.multiple_of(own_g * GR + y * RT, RT), RT)
        columns = pl.ds(pl.multiple_of(128 * own_k, 128), 128)
        goal = target[rows, columns]
        wait(zin.at[pl.ds(0, NZ - 1)], recv_sem.at[S_ZOUT])
        below = jnp.zeros((RT, 128), F32)
        errors = []
        for p in range(NZ):
            rout[p, 0] = below.astype(BF16)
            errors.append(number[p] * (goal - below) - zin[p, 1].astype(F32))
            below = below + zin[p, 0].astype(F32)
        above = jnp.zeros((RT, 128), F32)
        for p in range(NZ - 1, -1, -1):
            rout[p, 1] = above.astype(BF16)
            above = above + errors[p]
        for d in Z_ORDER:
            to = lax.rem(z + d, NZ)
            send(rout.at[to], rin.at[own_g, own_k], S_RET, recv_sem.at[S_RET + own_g], to * NY + y, row)
        rin[own_g, own_k] = rout[z]

    lane = lax.broadcasted_iota(jnp.int32, (1, 128), 1)
    squares = [jnp.zeros((RT, WIDTH), F32) for j in range(NY)]
    ended = jnp.zeros((RT, WIDTH), F32)
    for g in range(GROUPS):

        @pl.when(own_g == g)
        def _():
            wait(rin.at[g, pl.ds(0, TILES - 1)], recv_sem.at[S_RET + g])

        @pl.when(own_g != g)
        def _():
            wait(rin.at[g], recv_sem.at[S_RET + g])

        below = jnp.concatenate([rin[g, k, 0] for k in range(TILES)], axis=1).astype(F32)
        suffix = jnp.concatenate([rin[g, k, 1] for k in range(TILES)], axis=1).astype(F32)
        running = band(target, g, y)[...] - below
        inclusive = []
        for j in range(NY):
            running = running - ybuf[g, j].astype(F32)
            inclusive.append(running)
        for j in range(NY - 1, -1, -1):
            suffix = suffix + ends_at[j] * inclusive[j]
            gout[g, j] = (-2.0 / B * suffix).astype(BF16)
        for d in Y_ORDER:
            to = lax.rem(y + d, NY)
            send(gout.at[g, to], band(pgrad, g, y), S_GRAD, recv_sem.at[S_GRAD + g], z * NY + to, row)
        band(pgrad, g, y)[...] = gout[g, y]
        for j in range(NY):
            squares[j] = squares[j] + inclusive[j] * inclusive[j]
            ended = ended + ends_at[j] * inclusive[j]
    pending.append((gout.at[:, pl.ds(0, NY - 1)], S_GRAD))

    loss_row = jnp.zeros((1, 128), F32)
    for j in range(NY):
        square = jnp.sum(jnp.sum(squares[j], axis=0, keepdims=True), axis=1, keepdims=True)
        mark = jnp.zeros((1, 128), F32)
        for k in range(PREFIXES):
            mark = mark + jnp.where(lane == k, ends[j][k], 0.0)
        loss_row = loss_row + square * mark
    bias_row = -2.0 / B * jnp.sum(ended, axis=0, keepdims=True)
    lbuf[row] = jnp.broadcast_to(loss_row, (8, 128))
    for xx, cc in row_peers():
        send(lbuf.at[row], lbuf.at[row], S_LOSS, recv_sem.at[S_LOSS], lat, xx * NC + cc)
    pending.append((lbuf.at[pl.ds(0, ROWS - 1)], S_LOSS))

    for g in range(GROUPS):
        wait(gout.at[g, pl.ds(0, NY - 1)], recv_sem.at[S_GRAD + g])
        code_out[group(g)] = jnp.dot(pgrad[group(g)], wdec_t[...], preferred_element_type=F32).astype(BF16)
        for xx, cc in row_peers():
            send(block(code_out, g, xx, cc), code_in.at[g, row], S_CODE, recv_sem.at[S_CODE + g], lat, xx * NC + cc)
        code_in[g, row] = block(code_out, g, x, c)[...]
    pending.append((code_in.at[:, pl.ds(0, ROWS - 1)], S_CODE))

    gdec[...] = lax.dot_general(
        codes[...], pgrad[...], (((0,), (0,)), ((), ())), preferred_element_type=F32
    ).astype(BF16)
    put_dec = pltpu.make_async_copy(gdec, grad_dec, local_sem.at[L_GDEC])
    put_dec.start()

    row_sum = jnp.zeros((8, CB), F32)
    for g in range(GROUPS):
        wait(code_in.at[g, pl.ds(0, ROWS - 1)], recv_sem.at[S_CODE + g])
        code_grad = code_in[g, 0].astype(F32)
        for r in range(1, ROWS):
            code_grad = code_grad + code_in[g, r].astype(F32)
        pre_grad = code_grad * sig[g]
        row_sum = row_sum + (pre_grad[0:8] + pre_grad[8:16])
        block(pgb, g, x, c)[...] = pre_grad.astype(BF16)
    sums[row] = row_sum
    for xx, cc in row_peers():
        send(sums.at[row], sums.at[row], S_SUM, recv_sem.at[S_SUM], lat, xx * NC + cc)
    for g in range(GROUPS):
        for xx, cc in row_peers():
            send(block(pgb, g, x, c), block(pgb, g, x, c), S_PG, recv_sem.at[S_PG], lat, xx * NC + cc)
    pending.append((sums.at[pl.ds(0, ROWS - 1)], S_SUM))
    pending.append((code_in.at[:, pl.ds(0, ROWS - 1)], S_PG))

    wait(sums.at[pl.ds(0, ROWS - 1)], recv_sem.at[S_SUM])
    halves = []
    for cc in range(NC):
        half = sums[cc]
        for xx in range(1, NX):
            half = half + sums[xx * NC + cc]
        halves.append(jnp.sum(half, axis=0, keepdims=True))
    benc = jnp.concatenate(halves, axis=1)
    grad_benc[...] = benc
    high = benc.astype(BF16)
    middle = (benc - high.astype(F32)).astype(BF16)
    low = (benc - high.astype(F32) - middle.astype(F32)).astype(BF16)
    three = jnp.concatenate([high, middle, low, jnp.zeros((13, LAT), BF16)], axis=0)
    term = jnp.dot(three, wenc_t[...], preferred_element_type=F32)
    bias_row = bias_row - (term[0:1] + (term[1:2] + term[2:3]))
    wait(lbuf.at[pl.ds(0, ROWS - 1)], recv_sem.at[S_LOSS])
    loss_all = lbuf[0, 0:1]
    for r in range(1, ROWS):
        loss_all = loss_all + lbuf[r, 0:1]
    pieces = [bias_row[:, 128 * k : 128 * k + 128] for k in range(4)]
    by[y] = jnp.concatenate(pieces + [loss_all, jnp.zeros((3, 128), F32)], axis=0)
    for d in Y_ORDER:
        send(by.at[y], by.at[y], S_BY, recv_sem.at[S_BY], z * NY + lax.rem(y + d, NY), row)
    pending.append((by.at[pl.ds(0, NY - 1)], S_BY))

    wait(by.at[pl.ds(0, NY - 1)], recv_sem.at[S_BY])
    bz[z] = (by[0] + by[1]) + (by[2] + by[3])
    for d in Z_ORDER:
        to = lax.rem(z + d, NZ)
        send(bz.at[z], bz.at[z], S_BZ, recv_sem.at[S_BZ], to * NY + y, row)
    pending.append((bz.at[pl.ds(0, NZ - 1)], S_BZ))

    wait(code_in.at[:, pl.ds(0, ROWS - 1)], recv_sem.at[S_PG])
    genc[...] = lax.dot_general(
        centred[...], pgb[...], (((0,), (0,)), ((), ())), preferred_element_type=F32
    ).astype(BF16)
    put_enc = pltpu.make_async_copy(genc, grad_enc, local_sem.at[L_GENC])
    put_enc.start()

    @pl.when(is_owner)
    def _():
        wait(zin.at[pl.ds(0, GROUPS * TILES - 1)], send_sem.at[S_ZOUT])
        wait(rout.at[pl.ds(0, NZ - 1)], send_sem.at[S_RET])

    @pl.when(jnp.logical_not(is_owner))
    def _():
        wait(zin.at[pl.ds(0, GROUPS * TILES)], send_sem.at[S_ZOUT])

    for ref, sem in pending:
        wait(ref, send_sem.at[sem])
    put_dec.wait()
    put_enc.wait()
    wait(bz.at[pl.ds(0, NZ - 1)], recv_sem.at[S_BZ])
    everything = bz[0]
    for p in range(1, NZ):
        everything = everything + bz[p]
    tail[...] = everything


def finish(genc, benc, gdec, tail, grad_enc, grad_benc, grad_dec, grad_bdec, losses, sem):
    put_enc = pltpu.make_async_copy(genc, grad_enc, sem.at[0])
    put_dec = pltpu.make_async_copy(gdec, grad_dec, sem.at[1])
    put_enc.start()
    put_dec.start()
    grad_benc[...] = benc[...].reshape(LAT)
    grad_bdec[...] = tail[0:4].reshape(WIDTH)
    losses[...] = (tail[4] * (1.0 / (B * WIDTH * ROWS)))[0:PREFIXES]
    put_enc.wait()
    put_dec.wait()


def per_device(store, batch_rows, bounds, w_enc, b_enc, w_dec, b_dec):
    vmem, hbm = pl.BlockSpec(memory_space=pltpu.VMEM), pl.BlockSpec(memory_space=pl.ANY)
    operands = (store, batch_rows.reshape(1, B), bounds, w_enc, b_enc, w_dec, b_dec.reshape(1, WIDTH))
    genc, benc, gdec, tail = pl.pallas_call(
        kernel,
        out_shape=(
            jax.ShapeDtypeStruct((WIDTH, LAT), BF16),
            jax.ShapeDtypeStruct((1, LAT), F32),
            jax.ShapeDtypeStruct((LAT, WIDTH), BF16),
            jax.ShapeDtypeStruct((8, 128), F32),
        ),
        in_specs=[hbm] * 7,
        out_specs=(hbm, vmem, hbm, vmem),
        scratch_shapes=[
            pltpu.VMEM((1, B), jnp.int32),
            pltpu.SMEM((PREFIXES,), jnp.int32),
            pltpu.VMEM((LAT,), F32),
            pltpu.VMEM((1, LAT), F32),
            pltpu.VMEM((1, WIDTH), F32),
            pltpu.VMEM((WIDTH, LAT), BF16),
            pltpu.VMEM((LAT, WIDTH), BF16),
            pltpu.VMEM((LAT, WIDTH), BF16),
            pltpu.VMEM((WIDTH, LAT), BF16),
            pltpu.VMEM((B, STORE), BF16),
            pltpu.VMEM((STORE, WIDTH), BF16),
            pltpu.VMEM((B, WIDTH), F32),
            pltpu.VMEM((B, WIDTH), BF16),
            pltpu.VMEM((B, LAT), BF16),
            pltpu.VMEM((GROUPS, ROWS, RT, CB), BF16),
            pltpu.VMEM((GROUPS, RT, CB), F32),
            pltpu.VMEM((B, LAT), BF16),
            pltpu.VMEM((B, WIDTH), BF16),
            pltpu.VMEM((GROUPS, NY, RT, WIDTH), BF16),
            pltpu.VMEM((GROUPS, TILES, 2, RT, 128), BF16),
            pltpu.VMEM((NZ, 2, RT, 128), BF16),
            pltpu.VMEM((NZ, 2, RT, 128), BF16),
            pltpu.VMEM((GROUPS, TILES, 2, RT, 128), BF16),
            pltpu.VMEM((GROUPS, NY, RT, WIDTH), BF16),
            pltpu.VMEM((B, WIDTH), BF16),
            pltpu.VMEM((B, LAT), BF16),
            pltpu.VMEM((GROUPS, ROWS, RT, CB), BF16),
            pltpu.VMEM((B, LAT), BF16),
            pltpu.VMEM((ROWS, 8, CB), F32),
            pltpu.VMEM((ROWS, 8, 128), F32),
            pltpu.VMEM((LAT, WIDTH), BF16),
            pltpu.VMEM((WIDTH, LAT), BF16),
            pltpu.VMEM((NY, 8, 128), F32),
            pltpu.VMEM((NZ, 8, 128), F32),
            pltpu.SemaphoreType.DMA((9,)),
            pltpu.SemaphoreType.DMA((25,)),
            pltpu.SemaphoreType.DMA((25,)),
            pltpu.SemaphoreType.REGULAR((2,)),
        ],
        compiler_params=pltpu.CompilerParams(
            collective_id=0, has_side_effects=True, vmem_limit_bytes=40 * 2**20
        ),
        name="sae_step",
    )(*(pltpu.with_memory_space_constraint(operand, pltpu.HBM) for operand in operands))
    return pl.pallas_call(
        finish,
        out_shape=(
            jax.ShapeDtypeStruct((WIDTH, LAT), BF16),
            jax.ShapeDtypeStruct((LAT,), F32),
            jax.ShapeDtypeStruct((LAT, WIDTH), BF16),
            jax.ShapeDtypeStruct((WIDTH,), F32),
            jax.ShapeDtypeStruct((PREFIXES,), F32),
        ),
        in_specs=[hbm, vmem, hbm, vmem],
        out_specs=(hbm, vmem, hbm, vmem, vmem),
        scratch_shapes=[pltpu.SemaphoreType.DMA((2,))],
        compiler_params=pltpu.CompilerParams(vmem_limit_bytes=40 * 2**20),
        name="sae_finish",
    )(genc, benc, gdec, tail)


def solution(mesh):
    return jax.shard_map(
        per_device,
        mesh=mesh,
        in_specs=(P("row", None), P(), P(), P("row", "lat"), P("lat"), P("lat", "row"), P("row")),
        out_specs=(P("row", "lat"), P("lat"), P("lat", "row"), P("row"), P()),
        check_vma=False,
    )
```

time: 89 us -> 74.3 us (0.83)
  local copies, waits for them, and re-layouts: 6.98 us -> 0 us
  Pallas kernels: 79.8 us -> 73.6 us
  other arithmetic: 1.12 us -> 0 us
    pallas_call x1, Pallas kernels: 79.8 us -> 71.8 us  [per_device(): pl.pallas_call(kernel, out_shape=(jax.ShapeDtypeStruct((WIDTH, LAT), BF16...]
    unnamed x14 -> x0, local copies, waits for them, and re-layouts: 5.71 us -> none
    pallas_call x0 -> x1, Pallas kernels: none -> 1.74 us  [per_device(): pl.pallas_call(finish, out_shape=(jax.ShapeDtypeStruct((WIDTH, LAT), BF16...]
    reshape x2 -> x0, local copies, waits for them, and re-layouts: 1.27 us -> none  [the longest x1 0.69 us: per_device(): b_enc.reshape(1, LAT)]
where the time goes in v2:
time: 74.3 us; the launch traced here: 74.2 us
  Pallas kernels  73.6 us (99%)
    pallas_call x1, Pallas kernels, per_device(): pl.pallas_call(kernel, out_shape=(jax.ShapeDtypeStruct((WIDTH, LAT), BF16...  71.8 us
    pallas_call x1, Pallas kernels, per_device(): pl.pallas_call(finish, out_shape=(jax.ShapeDtypeStruct((WIDTH, LAT), BF16...  1.74 us

profile of v2, /device:TPU:1, one launch (start us, length us, event | category | flops | bytes accessed | tf_op | source)
XLA Modules:
  0.0 74.2 jit_solution(16263385560264166089)
XLA Ops:
  0.6 71.8 %sae_step.1 = (bf16[512,768]{1,0:T(8,128)(2,1)S(1)}, f32[1,768]{1,0:T(1,128)S(1)}, bf16[768,512]{1,0:T(8,128)(2,1)S(1)}, f32[8,128]{1,0:T(8,128)S(1)}) custom-call(bf16[48,4096]{1,0:T(8,128)(2,1)} %store.1, s32[1,192]{1,0:T(1,128)} %bitcast.3, s32[5]{0:T(128)} %bounds_hbm.1, bf16[512,768]{1,0:T(8,128)(2,1)} %w_enc.1, f32[768]{0:T(1024)} %b_enc_hbm.1, ...), custom_call_target="tpu_custom_call" | custom-call | tf_op jit(solution)/shard_map/sae_step/pallas_call | solution.py:358
  72.5 1.7 %sae_finish.1 = (bf16[512,768]{1,0:T(8,128)(2,1)}, f32[768]{0:T(1024)}, bf16[768,512]{1,0:T(8,128)(2,1)}, f32[512]{0:T(512)}, f32[5]{0:T(128)}) custom-call(bf16[512,768]{1,0:T(8,128)(2,1)S(1)} %get-tuple-element.9.genc, f32[1,768]{1,0:T(1,128)S(1)} %get-tuple-element.10.benc, bf16[768,512]{1,0:T(8,128)(2,1)S(1)} %get-tuple-element.11.gdec, ...), custom_call_target="tpu_custom_call" | custom-call | tf_op jit(solution)/shard_map/sae_finish/pallas_call | solution.py:413

commit v3 on v2

--- a/solution.py
+++ b/solution.py
@@ -17,26 +17,27 @@
 GR = B // GROUPS
 RT = GR // NX
 CB = LAT // NC
-TILES = WIDTH // 128
+MEMBERS, CLUSTERS = 16, 4
 
 X_ORDER = ((2, 0), (2, 1), (1, 0), (1, 1), (3, 0), (3, 1), (0, 1))
 Z_ORDER = (8, 7, 9, 6, 10, 5, 11, 4, 12, 3, 13, 2, 14, 1, 15)
 Y_ORDER = (2, 1, 3)
 
 L_ENC, L_DEC, L_STORE, L_GDEC, L_GENC, L_ROWS, L_BENC, L_BDEC, L_BOUNDS = range(9)
-S_PRE, S_CODES, S_PART, S_RET, S_GRAD, S_CODE = range(0, 18, 3)
-S_STORE, S_ZOUT, S_PG, S_SUM, S_LOSS, S_BY, S_BZ = range(18, 25)
+S_PRE, S_CODES, S_PART, S_FAR, S_GRAD, S_CODE = range(0, 18, 3)
+S_STORE, S_PG, S_SUM, S_BY, S_BZ = range(18, 23)
 
 
 def kernel(
     store, batch_rows_hbm, bounds_hbm, w_enc, b_enc_hbm, w_dec, b_dec_hbm,
     grad_enc, grad_benc, grad_dec, tail,
-    batch_rows, bounds, b_enc_flat, b_enc, b_dec, wenc, wdec, wenc_t, wdec_t, picks, cols, target, centred, pre_out, pre_in, sig, codes, part_out, ybuf, zout, zin, rout, rin,
-    gout, pgrad, code_out, code_in, pgb, sums, lbuf, gdec, genc, by, bz,
+    batch_rows, bounds, b_enc_flat, b_enc, b_dec, wenc, wdec, wenc_t, wdec_t, slope, picks, cols, target, centred, pre_out, pre_in, sig, codes, part_out, parts, far,
+    grads, pgrad, code_out, code_in, pgb, sums, gdec, genc, by, bz,
     local_sem, send_sem, recv_sem, relay_sem,
 ):
     lat, row = lax.axis_index("lat"), lax.axis_index("row")
     z, y = lat // NY, lax.rem(lat, NY)
+    cluster, member = lat // MEMBERS, lax.rem(lat, MEMBERS)
     x, c = row // NC, lax.rem(row, NC)
 
     def row_peers():
@@ -57,6 +58,9 @@
 
     def band(ref, g, i):
         return ref.at[pl.ds(pl.multiple_of(g * GR + i * RT, RT), RT)]
+
+    def tile(ref, g, m):
+        return band(ref, g, lax.rem(m, NY)).at[:, pl.ds(pl.multiple_of(m // NY * 128, 128), 128)]
 
     def block(ref, g, xx, cc):
         return band(ref, g, xx).at[:, pl.ds(pl.multiple_of(cc * CB, CB), CB)]
@@ -124,7 +128,6 @@
     pending.append((pre_in.at[:, pl.ds(0, ROWS - 1)], S_PRE))
     relay()
     relay()
-    wenc_t[...] = wenc[...].T
     my_b_enc = b_enc[:, pl.ds(pl.multiple_of(c * CB, CB), CB)]
     for g in range(GROUPS):
         pre_in[g, row] = block(pre_out, g, x, c)[...]
@@ -142,119 +145,116 @@
 
     relay()
     relay(last=True)
-    wdec_t[...] = wdec[...].T
     for g in range(GROUPS):
         wait(pre_in.at[g, pl.ds(0, ROWS - 1)], recv_sem.at[S_CODES + g])
         part_out[group(g)] = jnp.dot(codes[group(g)], wdec[...], preferred_element_type=F32).astype(BF16)
-        for d in Y_ORDER:
-            to = lax.rem(y + d, NY)
-            send(band(part_out, g, to), ybuf.at[g, y], S_PART, recv_sem.at[S_PART + g], z * NY + to, row)
-        ybuf[g, y] = band(part_out, g, y)[...]
-    pending.append((ybuf.at[:, pl.ds(0, NY - 1)], S_PART))
+        for d in Z_ORDER:
+            to = lax.rem(member + d, MEMBERS)
+            send(
+                tile(part_out, g, to), parts.at[g, member], S_PART, recv_sem.at[S_PART + g],
+                cluster * MEMBERS + to, row,
+            )
+        parts[g, member] = tile(part_out, g, member)[...]
+    pending.append((parts.at[:, pl.ds(0, MEMBERS - 1)], S_PART))
+
+    soft = codes[...].astype(F32)
+    slope[...] = jnp.where(soft < 0.01, soft * (1.0 - soft * (0.5 - soft * (1.0 / 6.0))), 1.0 - jnp.exp(-soft))
+    wdec_t[...] = wdec[...].T
+    wenc_t[...] = wenc[...].T
 
     ends = [
-        [jnp.where(bounds[k] == z * NY + j + 1, 1.0, 0.0).astype(F32) for k in range(PREFIXES)] for j in range(NY)
+        [jnp.where(bounds[k] == cluster * MEMBERS + j + 1, 1.0, 0.0).astype(F32) for k in range(PREFIXES)]
+        for j in range(MEMBERS)
     ]
-    ends_at = [sum(ends[j][1:], ends[j][0]) for j in range(NY)]
-    number = []
-    for p in range(NZ):
-        inside = [jnp.logical_and(bounds[k] > p * NY, bounds[k] <= (p + 1) * NY) for k in range(PREFIXES)]
+    ends_at = [sum(ends[j][1:], ends[j][0]) for j in range(MEMBERS)]
+    number, lower, higher = [], [], []
+    for h in range(CLUSTERS):
+        inside = [
+            jnp.logical_and(bounds[k] > h * MEMBERS, bounds[k] <= (h + 1) * MEMBERS) for k in range(PREFIXES)
+        ]
         counts = [jnp.where(one, 1.0, 0.0).astype(F32) for one in inside]
         number.append(sum(counts[1:], counts[0]))
-    for g in range(GROUPS):
-        wait(ybuf.at[g, pl.ds(0, NY - 1)], recv_sem.at[S_PART + g])
-        total = ybuf[g, 0].astype(F32)
+        lower.append(jnp.where(h < cluster, 1.0, 0.0).astype(F32))
+        higher.append(jnp.where(h > cluster, 1.0, 0.0).astype(F32))
+
+    for g in range(GROUPS):
+        wait(parts.at[g, pl.ds(0, MEMBERS - 1)], recv_sem.at[S_PART + g])
+        total = parts[g, 0].astype(F32)
         cut = ends_at[0] * total
-        for j in range(1, NY):
-            total = total + ybuf[g, j].astype(F32)
+        for j in range(1, MEMBERS):
+            total = total + parts[g, j].astype(F32)
             cut = cut + ends_at[j] * total
-        for k in range(TILES):
-            zout[g, k, 0] = total[:, 128 * k : 128 * k + 128].astype(BF16)
-            zout[g, k, 1] = cut[:, 128 * k : 128 * k + 128].astype(BF16)
-        for d in range(TILES):
-            k = lax.rem(z // 4 + (2, 1, 3, 0)[d], TILES)
-            to = 4 * k + g
-
-            @pl.when(to != z)
-            def _():
-                send(zout.at[g, k], zin.at[z], S_ZOUT, recv_sem.at[S_ZOUT], to * NY + y, row)
-
-    own_g, own_k = lax.rem(z, 4), z // 4
-    is_owner = own_g < GROUPS
-
-    @pl.when(is_owner)
-    def _():
-        zin[z] = zout[own_g, own_k]
-        rows = pl.ds(pl.multiple_of(own_g * GR + y * RT, RT), RT)
-        columns = pl.ds(pl.multiple_of(128 * own_k, 128), 128)
-        goal = target[rows, columns]
-        wait(zin.at[pl.ds(0, NZ - 1)], recv_sem.at[S_ZOUT])
+        far[g, cluster, 0] = total.astype(BF16)
+        far[g, cluster, 1] = cut.astype(BF16)
+        for d in (2, 1, 3):
+            to = lax.rem(cluster + d, CLUSTERS) * MEMBERS + member
+            send(far.at[g, cluster], far.at[g, cluster], S_FAR, recv_sem.at[S_FAR + g], to, row)
+    pending.append((far.at[:, pl.ds(0, CLUSTERS - 1)], S_FAR))
+
+    errors = []
+    for g in range(GROUPS):
+        wait(far.at[g, pl.ds(0, CLUSTERS - 1)], recv_sem.at[S_FAR + g])
+        goal = tile(target, g, member)[...]
         below = jnp.zeros((RT, 128), F32)
-        errors = []
-        for p in range(NZ):
-            rout[p, 0] = below.astype(BF16)
-            errors.append(number[p] * (goal - below) - zin[p, 1].astype(F32))
-            below = below + zin[p, 0].astype(F32)
-        above = jnp.zeros((RT, 128), F32)
-        for p in range(NZ - 1, -1, -1):
-            rout[p, 1] = above.astype(BF16)
-            above = above + errors[p]
+        running, suffix = goal, jnp.zeros((RT, 128), F32)
+        for h in range(CLUSTERS):
+            total = far[g, h, 0].astype(F32)
+            suffix = suffix + higher[h] * (number[h] * (goal - below) - far[g, h, 1].astype(F32))
+            running = running - lower[h] * total
+            below = below + total
+        inclusive = []
+        for j in range(MEMBERS):
+            running = running - parts[g, j].astype(F32)
+            inclusive.append(running)
+        for j in range(MEMBERS - 1, -1, -1):
+            suffix = suffix + ends_at[j] * inclusive[j]
+            grads[g, j] = (-2.0 / B * suffix).astype(BF16)
         for d in Z_ORDER:
-            to = lax.rem(z + d, NZ)
-            send(rout.at[to], rin.at[own_g, own_k], S_RET, recv_sem.at[S_RET + own_g], to * NY + y, row)
-        rin[own_g, own_k] = rout[z]
+            to = lax.rem(member + d, MEMBERS)
+            send(
+                grads.at[g, to], tile(pgrad, g, member), S_GRAD, recv_sem.at[S_GRAD + g],
+                cluster * MEMBERS + to, row,
+            )
+        tile(pgrad, g, member)[...] = grads[g, member]
+        for k in range(PREFIXES):
+            error = ends[0][k] * inclusive[0]
+            for j in range(1, MEMBERS):
+                error = error + ends[j][k] * inclusive[j]
+            if g == 0:
+                errors.append([error])
+            else:
+                errors[k].append(error)
+    pending.append((grads.at[:, pl.ds(0, MEMBERS - 1)], S_GRAD))
 
     lane = lax.broadcasted_iota(jnp.int32, (1, 128), 1)
-    squares = [jnp.zeros((RT, WIDTH), F32) for j in range(NY)]
-    ended = jnp.zeros((RT, WIDTH), F32)
-    for g in range(GROUPS):
-
-        @pl.when(own_g == g)
-        def _():
-            wait(rin.at[g, pl.ds(0, TILES - 1)], recv_sem.at[S_RET + g])
-
-        @pl.when(own_g != g)
-        def _():
-            wait(rin.at[g], recv_sem.at[S_RET + g])
-
-        below = jnp.concatenate([rin[g, k, 0] for k in range(TILES)], axis=1).astype(F32)
-        suffix = jnp.concatenate([rin[g, k, 1] for k in range(TILES)], axis=1).astype(F32)
-        running = band(target, g, y)[...] - below
-        inclusive = []
-        for j in range(NY):
-            running = running - ybuf[g, j].astype(F32)
-            inclusive.append(running)
-        for j in range(NY - 1, -1, -1):
-            suffix = suffix + ends_at[j] * inclusive[j]
-            gout[g, j] = (-2.0 / B * suffix).astype(BF16)
-        for d in Y_ORDER:
-            to = lax.rem(y + d, NY)
-            send(gout.at[g, to], band(pgrad, g, y), S_GRAD, recv_sem.at[S_GRAD + g], z * NY + to, row)
-        band(pgrad, g, y)[...] = gout[g, y]
-        for j in range(NY):
-            squares[j] = squares[j] + inclusive[j] * inclusive[j]
-            ended = ended + ends_at[j] * inclusive[j]
-    pending.append((gout.at[:, pl.ds(0, NY - 1)], S_GRAD))
-
-    loss_row = jnp.zeros((1, 128), F32)
-    for j in range(NY):
-        square = jnp.sum(jnp.sum(squares[j], axis=0, keepdims=True), axis=1, keepdims=True)
-        mark = jnp.zeros((1, 128), F32)
-        for k in range(PREFIXES):
-            mark = mark + jnp.where(lane == k, ends[j][k], 0.0)
-        loss_row = loss_row + square * mark
-    bias_row = -2.0 / B * jnp.sum(ended, axis=0, keepdims=True)
-    lbuf[row] = jnp.broadcast_to(loss_row, (8, 128))
-    for xx, cc in row_peers():
-        send(lbuf.at[row], lbuf.at[row], S_LOSS, recv_sem.at[S_LOSS], lat, xx * NC + cc)
-    pending.append((lbuf.at[pl.ds(0, ROWS - 1)], S_LOSS))
-
-    for g in range(GROUPS):
-        wait(gout.at[g, pl.ds(0, NY - 1)], recv_sem.at[S_GRAD + g])
-        code_out[group(g)] = jnp.dot(pgrad[group(g)], wdec_t[...], preferred_element_type=F32).astype(BF16)
+    loss_row, ended = jnp.zeros((1, 128), F32), jnp.zeros((RT, 128), F32)
+    for k in range(PREFIXES):
+        squares = jnp.zeros((RT, 128), F32)
+        for error in errors[k]:
+            squares = squares + error * error
+            ended = ended + error
+        square = jnp.sum(jnp.sum(squares, axis=0, keepdims=True), axis=1, keepdims=True)
+        loss_row = loss_row + jnp.where(lane == k, square, 0.0)
+    ended_row = -2.0 / B * jnp.sum(ended, axis=0, keepdims=True)
+
+    down = jnp.zeros((8, LAT), F32)
+    for g in range(GROUPS):
+        wait(grads.at[g, pl.ds(0, MEMBERS - 1)], recv_sem.at[S_GRAD + g])
+        partial = jnp.dot(pgrad[group(g)], wdec_t[...], preferred_element_type=F32)
+        code_out[group(g)] = partial.astype(BF16)
+        products = partial * slope[group(g)]
+        for i in range(0, GR, 8):
+            down = down + products[i : i + 8]
+        if g == GROUPS - 1:
+            benc = jnp.sum(down, axis=0, keepdims=True)
+            pieces = [benc[:, 128 * k : 128 * k + 128] for k in range(LAT // 128)]
+            sums[row] = jnp.concatenate(pieces + [loss_row, jnp.zeros((1, 128), F32)], axis=0)
+            for xx, cc in row_peers():
+                send(sums.at[row], sums.at[row], S_SUM, recv_sem.at[S_SUM], lat, xx * NC + cc)
         for xx, cc in row_peers():
             send(block(code_out, g, xx, cc), code_in.at[g, row], S_CODE, recv_sem.at[S_CODE + g], lat, xx * NC + cc)
         code_in[g, row] = block(code_out, g, x, c)[...]
+    pending.append((sums.at[pl.ds(0, ROWS - 1)], S_SUM))
     pending.append((code_in.at[:, pl.ds(0, ROWS - 1)], S_CODE))
 
     gdec[...] = lax.dot_general(
@@ -263,48 +263,40 @@
     put_dec = pltpu.make_async_copy(gdec, grad_dec, local_sem.at[L_GDEC])
     put_dec.start()
 
-    row_sum = jnp.zeros((8, CB), F32)
-    for g in range(GROUPS):
+    def own_code_grad(g):
         wait(code_in.at[g, pl.ds(0, ROWS - 1)], recv_sem.at[S_CODE + g])
         code_grad = code_in[g, 0].astype(F32)
         for r in range(1, ROWS):
             code_grad = code_grad + code_in[g, r].astype(F32)
-        pre_grad = code_grad * sig[g]
-        row_sum = row_sum + (pre_grad[0:8] + pre_grad[8:16])
-        block(pgb, g, x, c)[...] = pre_grad.astype(BF16)
-    sums[row] = row_sum
-    for xx, cc in row_peers():
-        send(sums.at[row], sums.at[row], S_SUM, recv_sem.at[S_SUM], lat, xx * NC + cc)
-    for g in range(GROUPS):
+        block(pgb, g, x, c)[...] = (code_grad * sig[g]).astype(BF16)
         for xx, cc in row_peers():
             send(block(pgb, g, x, c), block(pgb, g, x, c), S_PG, recv_sem.at[S_PG], lat, xx * NC + cc)
-    pending.append((sums.at[pl.ds(0, ROWS - 1)], S_SUM))
-    pending.append((code_in.at[:, pl.ds(0, ROWS - 1)], S_PG))
+
+    for g in range(GROUPS - 1):
+        own_code_grad(g)
 
     wait(sums.at[pl.ds(0, ROWS - 1)], recv_sem.at[S_SUM])
-    halves = []
-    for cc in range(NC):
-        half = sums[cc]
-        for xx in range(1, NX):
-            half = half + sums[xx * NC + cc]
-        halves.append(jnp.sum(half, axis=0, keepdims=True))
-    benc = jnp.concatenate(halves, axis=1)
-    grad_benc[...] = benc
+    summed = sums[0]
+    for r in range(1, ROWS):
+        summed = summed + sums[r]
+    benc = jnp.concatenate([summed[k : k + 1] for k in range(LAT // 128)], axis=1)
     high = benc.astype(BF16)
     middle = (benc - high.astype(F32)).astype(BF16)
     low = (benc - high.astype(F32) - middle.astype(F32)).astype(BF16)
     three = jnp.concatenate([high, middle, low, jnp.zeros((13, LAT), BF16)], axis=0)
     term = jnp.dot(three, wenc_t[...], preferred_element_type=F32)
-    bias_row = bias_row - (term[0:1] + (term[1:2] + term[2:3]))
-    wait(lbuf.at[pl.ds(0, ROWS - 1)], recv_sem.at[S_LOSS])
-    loss_all = lbuf[0, 0:1]
-    for r in range(1, ROWS):
-        loss_all = loss_all + lbuf[r, 0:1]
-    pieces = [bias_row[:, 128 * k : 128 * k + 128] for k in range(4)]
-    by[y] = jnp.concatenate(pieces + [loss_all, jnp.zeros((3, 128), F32)], axis=0)
+    term = term[0:1] + (term[1:2] + term[2:3])
+    pieces = [
+        jnp.where(member // NY == k, ended_row, 0.0) - term[:, 128 * k : 128 * k + 128] for k in range(WIDTH // 128)
+    ]
+    by[y] = jnp.concatenate(pieces + [summed[6:7], jnp.zeros((3, 128), F32)], axis=0)
     for d in Y_ORDER:
         send(by.at[y], by.at[y], S_BY, recv_sem.at[S_BY], z * NY + lax.rem(y + d, NY), row)
     pending.append((by.at[pl.ds(0, NY - 1)], S_BY))
+    grad_benc[...] = benc
+
+    own_code_grad(GROUPS - 1)
+    pending.append((code_in.at[:, pl.ds(0, ROWS - 1)], S_PG))
 
     wait(by.at[pl.ds(0, NY - 1)], recv_sem.at[S_BY])
     bz[z] = (by[0] + by[1]) + (by[2] + by[3])
@@ -319,15 +311,6 @@
     ).astype(BF16)
     put_enc = pltpu.make_async_copy(genc, grad_enc, local_sem.at[L_GENC])
     put_enc.start()
-
-    @pl.when(is_owner)
-    def _():
-        wait(zin.at[pl.ds(0, GROUPS * TILES - 1)], send_sem.at[S_ZOUT])
-        wait(rout.at[pl.ds(0, NZ - 1)], send_sem.at[S_RET])
-
-    @pl.when(jnp.logical_not(is_owner))
-    def _():
-        wait(zin.at[pl.ds(0, GROUPS * TILES)], send_sem.at[S_ZOUT])
 
     for ref, sem in pending:
         wait(ref, send_sem.at[sem])
@@ -375,6 +358,7 @@
             pltpu.VMEM((LAT, WIDTH), BF16),
             pltpu.VMEM((LAT, WIDTH), BF16),
             pltpu.VMEM((WIDTH, LAT), BF16),
+            pltpu.VMEM((B, LAT), F32),
             pltpu.VMEM((B, STORE), BF16),
             pltpu.VMEM((STORE, WIDTH), BF16),
             pltpu.VMEM((B, WIDTH), F32),
@@ -384,25 +368,21 @@
             pltpu.VMEM((GROUPS, RT, CB), F32),
             pltpu.VMEM((B, LAT), BF16),
             pltpu.VMEM((B, WIDTH), BF16),
-            pltpu.VMEM((GROUPS, NY, RT, WIDTH), BF16),
-            pltpu.VMEM((GROUPS, TILES, 2, RT, 128), BF16),
-            pltpu.VMEM((NZ, 2, RT, 128), BF16),
-            pltpu.VMEM((NZ, 2, RT, 128), BF16),
-            pltpu.VMEM((GROUPS, TILES, 2, RT, 128), BF16),
-            pltpu.VMEM((GROUPS, NY, RT, WIDTH), BF16),
+            pltpu.VMEM((GROUPS, MEMBERS, RT, 128), BF16),
+            pltpu.VMEM((GROUPS, CLUSTERS, 2, RT, 128), BF16),
+            pltpu.VMEM((GROUPS, MEMBERS, RT, 128), BF16),
             pltpu.VMEM((B, WIDTH), BF16),
             pltpu.VMEM((B, LAT), BF16),
             pltpu.VMEM((GROUPS, ROWS, RT, CB), BF16),
             pltpu.VMEM((B, LAT), BF16),
-            pltpu.VMEM((ROWS, 8, CB), F32),
             pltpu.VMEM((ROWS, 8, 128), F32),
             pltpu.VMEM((LAT, WIDTH), BF16),
             pltpu.VMEM((WIDTH, LAT), BF16),
             pltpu.VMEM((NY, 8, 128), F32),
             pltpu.VMEM((NZ, 8, 128), F32),
             pltpu.SemaphoreType.DMA((9,)),
-            pltpu.SemaphoreType.DMA((25,)),
-            pltpu.SemaphoreType.DMA((25,)),
+            pltpu.SemaphoreType.DMA((23,)),
+            pltpu.SemaphoreType.DMA((23,)),
             pltpu.SemaphoreType.REGULAR((2,)),
         ],
         compiler_params=pltpu.CompilerParams(

time: 74.3 us -> 66 us (0.89)
  Pallas kernels: 73.6 us -> 65.3 us
    pallas_call x1, Pallas kernels: 71.8 us -> 63.5 us  [per_device(): pl.pallas_call(kernel, out_shape=(jax.ShapeDtypeStruct((WIDTH, LAT), BF16...]
where the time goes in v3:
time: 66 us; the launch traced here: 65.9 us
  Pallas kernels  65.3 us (99%)
    pallas_call x1, Pallas kernels, per_device(): pl.pallas_call(kernel, out_shape=(jax.ShapeDtypeStruct((WIDTH, LAT), BF16...  63.5 us
    pallas_call x1, Pallas kernels, per_device(): pl.pallas_call(finish, out_shape=(jax.ShapeDtypeStruct((WIDTH, LAT), BF16...  1.74 us

profile of v3, /device:TPU:1, one launch (start us, length us, event | category | flops | bytes accessed | tf_op | source)
XLA Modules:
  0.0 65.9 jit_solution(11197628108941488925)
XLA Ops:
  0.6 63.5 %sae_step.1 = (bf16[512,768]{1,0:T(8,128)(2,1)S(1)}, f32[1,768]{1,0:T(1,128)S(1)}, bf16[768,512]{1,0:T(8,128)(2,1)S(1)}, f32[8,128]{1,0:T(8,128)S(1)}) custom-call(bf16[48,4096]{1,0:T(8,128)(2,1)} %store.1, s32[1,192]{1,0:T(1,128)} %bitcast.3, s32[5]{0:T(128)} %bounds_hbm.1, bf16[512,768]{1,0:T(8,128)(2,1)} %w_enc.1, f32[768]{0:T(1024)} %b_enc_hbm.1, ...), custom_call_target="tpu_custom_call" | custom-call | tf_op jit(solution)/shard_map/sae_step/pallas_call | solution.py:341
  64.2 1.7 %sae_finish.1 = (bf16[512,768]{1,0:T(8,128)(2,1)}, f32[768]{0:T(1024)}, bf16[768,512]{1,0:T(8,128)(2,1)}, f32[512]{0:T(512)}, f32[5]{0:T(128)}) custom-call(bf16[512,768]{1,0:T(8,128)(2,1)S(1)} %get-tuple-element.9.genc, f32[1,768]{1,0:T(1,128)S(1)} %get-tuple-element.10.benc, bf16[768,512]{1,0:T(8,128)(2,1)S(1)} %get-tuple-element.11.gdec, ...), custom_call_target="tpu_custom_call" | custom-call | tf_op jit(solution)/shard_map/sae_finish/pallas_call | solution.py:393

commit v4 on v3

--- a/solution.py
+++ b/solution.py
@@ -17,27 +17,42 @@
 GR = B // GROUPS
 RT = GR // NX
 CB = LAT // NC
-MEMBERS, CLUSTERS = 16, 4
+MEMBERS, CLUSTERS, OWNERS = 16, 4, 8
+HALF = WIDTH // 2
 
 X_ORDER = ((2, 0), (2, 1), (1, 0), (1, 1), (3, 0), (3, 1), (0, 1))
 Z_ORDER = (8, 7, 9, 6, 10, 5, 11, 4, 12, 3, 13, 2, 14, 1, 15)
 Y_ORDER = (2, 1, 3)
+L_ORDER = sorted(
+    ((dz, dy) for dz in range(NZ) for dy in range(NY) if dz or dy),
+    key=lambda d: -(min(d[0], NZ - d[0]) + min(d[1], NY - d[1])),
+)
+O_ORDER = (6, 2, 5, 7, 1, 3, 4, 0)
 
 L_ENC, L_DEC, L_STORE, L_GDEC, L_GENC, L_ROWS, L_BENC, L_BDEC, L_BOUNDS = range(9)
 S_PRE, S_CODES, S_PART, S_FAR, S_GRAD, S_CODE = range(0, 18, 3)
-S_STORE, S_PG, S_SUM, S_BY, S_BZ = range(18, 23)
+S_STORE, S_PG, S_SUM, S_BIAS, S_LROW, S_LY, S_LZ = range(18, 25)
+
+
+def ordered_sum(ref, count):
+    total = ref[0]
+    for i in range(1, count):
+        total = total + ref[i]
+    return total
 
 
 def kernel(
     store, batch_rows_hbm, bounds_hbm, w_enc, b_enc_hbm, w_dec, b_dec_hbm,
     grad_enc, grad_benc, grad_dec, tail,
-    batch_rows, bounds, b_enc_flat, b_enc, b_dec, wenc, wdec, wenc_t, wdec_t, slope, picks, cols, target, centred, pre_out, pre_in, sig, codes, part_out, parts, far,
-    grads, pgrad, code_out, code_in, pgb, sums, gdec, genc, by, bz,
+    batch_rows, bounds, b_enc_flat, b_enc, b_dec, wenc, wdec, wenc_t, wdec_t, slope, picks, cols, target, centred, pre_out, pre_in, sig, codes, part_out, parts, near, far,
+    grads, losses, ended, pgrad, code_out, code_in, pgb, sums, gdec, genc, biases, by_row, by_y, by_z,
     local_sem, send_sem, recv_sem, relay_sem,
 ):
     lat, row = lax.axis_index("lat"), lax.axis_index("row")
     z, y = lat // NY, lax.rem(lat, NY)
     cluster, member = lat // MEMBERS, lax.rem(lat, MEMBERS)
+    is_owner = jnp.logical_and(member >= NY, member < NY + OWNERS)
+    own = jnp.clip(member - NY, 0, OWNERS - 1)
     x, c = row // NC, lax.rem(row, NC)
 
     def row_peers():
@@ -59,8 +74,8 @@
     def band(ref, g, i):
         return ref.at[pl.ds(pl.multiple_of(g * GR + i * RT, RT), RT)]
 
-    def tile(ref, g, m):
-        return band(ref, g, lax.rem(m, NY)).at[:, pl.ds(pl.multiple_of(m // NY * 128, 128), 128)]
+    def part(ref, g, owner):
+        return band(ref, g, lax.rem(owner, NY)).at[:, pl.ds(pl.multiple_of(owner // NY * HALF, HALF), HALF)]
 
     def block(ref, g, xx, cc):
         return band(ref, g, xx).at[:, pl.ds(pl.multiple_of(cc * CB, CB), CB)]
@@ -148,98 +163,112 @@
     for g in range(GROUPS):
         wait(pre_in.at[g, pl.ds(0, ROWS - 1)], recv_sem.at[S_CODES + g])
         part_out[group(g)] = jnp.dot(codes[group(g)], wdec[...], preferred_element_type=F32).astype(BF16)
-        for d in Z_ORDER:
-            to = lax.rem(member + d, MEMBERS)
-            send(
-                tile(part_out, g, to), parts.at[g, member], S_PART, recv_sem.at[S_PART + g],
-                cluster * MEMBERS + to, row,
-            )
-        parts[g, member] = tile(part_out, g, member)[...]
-    pending.append((parts.at[:, pl.ds(0, MEMBERS - 1)], S_PART))
+        for d in O_ORDER:
+            to = lax.rem(own + d, OWNERS)
+
+            @pl.when(to + NY != member)
+            def _():
+                send(
+                    part(part_out, g, to), parts.at[g, member], S_PART, recv_sem.at[S_PART + g],
+                    cluster * MEMBERS + NY + to, row,
+                )
 
     soft = codes[...].astype(F32)
     slope[...] = jnp.where(soft < 0.01, soft * (1.0 - soft * (0.5 - soft * (1.0 / 6.0))), 1.0 - jnp.exp(-soft))
     wdec_t[...] = wdec[...].T
     wenc_t[...] = wenc[...].T
-
-    ends = [
-        [jnp.where(bounds[k] == cluster * MEMBERS + j + 1, 1.0, 0.0).astype(F32) for k in range(PREFIXES)]
-        for j in range(MEMBERS)
-    ]
-    ends_at = [sum(ends[j][1:], ends[j][0]) for j in range(MEMBERS)]
-    number, lower, higher = [], [], []
-    for h in range(CLUSTERS):
-        inside = [
-            jnp.logical_and(bounds[k] > h * MEMBERS, bounds[k] <= (h + 1) * MEMBERS) for k in range(PREFIXES)
+    losses[...] = jnp.zeros((1, 128), F32)
+    ended[...] = jnp.zeros((1, HALF), F32)
+
+    @pl.when(is_owner)
+    def _():
+        ends = [
+            [jnp.where(bounds[k] == cluster * MEMBERS + j + 1, 1.0, 0.0).astype(F32) for k in range(PREFIXES)]
+            for j in range(MEMBERS)
         ]
-        counts = [jnp.where(one, 1.0, 0.0).astype(F32) for one in inside]
-        number.append(sum(counts[1:], counts[0]))
-        lower.append(jnp.where(h < cluster, 1.0, 0.0).astype(F32))
-        higher.append(jnp.where(h > cluster, 1.0, 0.0).astype(F32))
-
-    for g in range(GROUPS):
-        wait(parts.at[g, pl.ds(0, MEMBERS - 1)], recv_sem.at[S_PART + g])
-        total = parts[g, 0].astype(F32)
-        cut = ends_at[0] * total
-        for j in range(1, MEMBERS):
-            total = total + parts[g, j].astype(F32)
-            cut = cut + ends_at[j] * total
-        far[g, cluster, 0] = total.astype(BF16)
-        far[g, cluster, 1] = cut.astype(BF16)
-        for d in (2, 1, 3):
-            to = lax.rem(cluster + d, CLUSTERS) * MEMBERS + member
-            send(far.at[g, cluster], far.at[g, cluster], S_FAR, recv_sem.at[S_FAR + g], to, row)
-    pending.append((far.at[:, pl.ds(0, CLUSTERS - 1)], S_FAR))
-
-    errors = []
-    for g in range(GROUPS):
-        wait(far.at[g, pl.ds(0, CLUSTERS - 1)], recv_sem.at[S_FAR + g])
-        goal = tile(target, g, member)[...]
-        below = jnp.zeros((RT, 128), F32)
-        running, suffix = goal, jnp.zeros((RT, 128), F32)
-        for h in range(CLUSTERS):
-            total = far[g, h, 0].astype(F32)
-            suffix = suffix + higher[h] * (number[h] * (goal - below) - far[g, h, 1].astype(F32))
-            running = running - lower[h] * total
-            below = below + total
-        inclusive = []
-        for j in range(MEMBERS):
-            running = running - parts[g, j].astype(F32)
-            inclusive.append(running)
-        for j in range(MEMBERS - 1, -1, -1):
-            suffix = suffix + ends_at[j] * inclusive[j]
-            grads[g, j] = (-2.0 / B * suffix).astype(BF16)
-        for d in Z_ORDER:
-            to = lax.rem(member + d, MEMBERS)
-            send(
-                grads.at[g, to], tile(pgrad, g, member), S_GRAD, recv_sem.at[S_GRAD + g],
-                cluster * MEMBERS + to, row,
-            )
-        tile(pgrad, g, member)[...] = grads[g, member]
+        ends_at = [sum(ends[j][1:], ends[j][0]) for j in range(MEMBERS)]
+        beyond = [jnp.where(bounds[k] > (cluster + 1) * MEMBERS, 1.0, 0.0).astype(F32) for k in range(PREFIXES)]
+        above = sum(beyond[1:], beyond[0])
+
+        totals = []
+        for g in range(GROUPS):
+            parts[g, member] = part(part_out, g, own)[...]
+            wait(parts.at[g, pl.ds(0, MEMBERS - 1)], recv_sem.at[S_PART + g])
+            total = parts[g, 0].astype(F32)
+            cut = ends_at[0] * total
+            for j in range(1, MEMBERS):
+                total = total + parts[g, j].astype(F32)
+                cut = cut + ends_at[j] * total
+            totals.append(total)
+            near[g, 0] = total.astype(BF16)
+            near[g, 1] = (cut + above * total).astype(BF16)
+            for d in (2, 1, 3):
+                to = lax.rem(cluster + d, CLUSTERS)
+                which = jnp.where(to < cluster, 1, 0)
+                send(
+                    near.at[g, which], far.at[g, d - 1], S_FAR, recv_sem.at[S_FAR + g],
+                    to * MEMBERS + member, row,
+                )
+
+        errors = [[] for k in range(PREFIXES)]
+        for g in range(GROUPS):
+            wait(far.at[g], recv_sem.at[S_FAR + g])
+            running = part(target, g, own)[...]
+            over = jnp.zeros((RT, HALF), F32)
+            for d in range(1, CLUSTERS):
+                from_lower = jnp.where(d <= cluster, 1.0, 0.0).astype(F32)
+                got = far[g, d - 1].astype(F32)
+                running = running - from_lower * got
+                over = over + (1.0 - from_lower) * got
+            suffix = above * (running - totals[g]) - over
+            inclusive = []
+            for j in range(MEMBERS):
+                running = running - parts[g, j].astype(F32)
+                inclusive.append(running)
+            for j in range(MEMBERS - 1, -1, -1):
+                suffix = suffix + ends_at[j] * inclusive[j]
+                grads[g, j] = (-2.0 / B * suffix).astype(BF16)
+            for d in Z_ORDER:
+                to = lax.rem(member + d, MEMBERS)
+                send(
+                    grads.at[g, to], part(pgrad, g, own), S_GRAD, recv_sem.at[S_GRAD + g],
+                    cluster * MEMBERS + to, row,
+                )
+            part(pgrad, g, own)[...] = grads[g, member]
+            for k in range(PREFIXES):
+                error = ends[0][k] * inclusive[0]
+                for j in range(1, MEMBERS):
+                    error = error + ends[j][k] * inclusive[j]
+                errors[k].append(error)
+
+        lane = lax.broadcasted_iota(jnp.int32, (1, 128), 1)
+        loss_row, all_errors = jnp.zeros((1, 128), F32), jnp.zeros((RT, HALF), F32)
         for k in range(PREFIXES):
-            error = ends[0][k] * inclusive[0]
-            for j in range(1, MEMBERS):
-                error = error + ends[j][k] * inclusive[j]
-            if g == 0:
-                errors.append([error])
-            else:
-                errors[k].append(error)
-    pending.append((grads.at[:, pl.ds(0, MEMBERS - 1)], S_GRAD))
-
-    lane = lax.broadcasted_iota(jnp.int32, (1, 128), 1)
-    loss_row, ended = jnp.zeros((1, 128), F32), jnp.zeros((RT, 128), F32)
-    for k in range(PREFIXES):
-        squares = jnp.zeros((RT, 128), F32)
-        for error in errors[k]:
-            squares = squares + error * error
-            ended = ended + error
-        square = jnp.sum(jnp.sum(squares, axis=0, keepdims=True), axis=1, keepdims=True)
-        loss_row = loss_row + jnp.where(lane == k, square, 0.0)
-    ended_row = -2.0 / B * jnp.sum(ended, axis=0, keepdims=True)
+            squares = jnp.zeros((RT, HALF), F32)
+            for error in errors[k]:
+                squares = squares + error * error
+                all_errors = all_errors + error
+            square = jnp.sum(jnp.sum(squares, axis=0, keepdims=True), axis=1, keepdims=True)
+            loss_row = loss_row + jnp.where(lane == k, square, 0.0)
+        losses[...] = loss_row
+        ended[...] = -2.0 / B * jnp.sum(all_errors, axis=0, keepdims=True)
+
+    by_row[row] = losses[...]
+    for xx, cc in row_peers():
+        send(by_row.at[row], by_row.at[row], S_LROW, recv_sem.at[S_LROW], lat, xx * NC + cc)
+    pending.append((by_row.at[pl.ds(0, ROWS - 1)], S_LROW))
 
     down = jnp.zeros((8, LAT), F32)
     for g in range(GROUPS):
-        wait(grads.at[g, pl.ds(0, MEMBERS - 1)], recv_sem.at[S_GRAD + g])
+
+        @pl.when(is_owner)
+        def _():
+            wait(grads.at[g, pl.ds(0, OWNERS - 1)], recv_sem.at[S_GRAD + g])
+
+        @pl.when(jnp.logical_not(is_owner))
+        def _():
+            wait(grads.at[g, pl.ds(0, OWNERS)], recv_sem.at[S_GRAD + g])
+
         partial = jnp.dot(pgrad[group(g)], wdec_t[...], preferred_element_type=F32)
         code_out[group(g)] = partial.astype(BF16)
         products = partial * slope[group(g)]
@@ -248,12 +277,18 @@
         if g == GROUPS - 1:
             benc = jnp.sum(down, axis=0, keepdims=True)
             pieces = [benc[:, 128 * k : 128 * k + 128] for k in range(LAT // 128)]
-            sums[row] = jnp.concatenate(pieces + [loss_row, jnp.zeros((1, 128), F32)], axis=0)
+            sums[row] = jnp.concatenate(pieces + [jnp.zeros((2, 128), F32)], axis=0)
             for xx, cc in row_peers():
                 send(sums.at[row], sums.at[row], S_SUM, recv_sem.at[S_SUM], lat, xx * NC + cc)
         for xx, cc in row_peers():
             send(block(code_out, g, xx, cc), code_in.at[g, row], S_CODE, recv_sem.at[S_CODE + g], lat, xx * NC + cc)
         code_in[g, row] = block(code_out, g, x, c)[...]
+        if g == 0:
+            wait(by_row.at[pl.ds(0, ROWS - 1)], recv_sem.at[S_LROW])
+            by_y[y] = ordered_sum(by_row, ROWS)
+            for d in Y_ORDER:
+                send(by_y.at[y], by_y.at[y], S_LY, recv_sem.at[S_LY], z * NY + lax.rem(y + d, NY), row)
+            pending.append((by_y.at[pl.ds(0, NY - 1)], S_LY))
     pending.append((sums.at[pl.ds(0, ROWS - 1)], S_SUM))
     pending.append((code_in.at[:, pl.ds(0, ROWS - 1)], S_CODE))
 
@@ -272,13 +307,16 @@
         for xx, cc in row_peers():
             send(block(pgb, g, x, c), block(pgb, g, x, c), S_PG, recv_sem.at[S_PG], lat, xx * NC + cc)
 
+    wait(by_y.at[pl.ds(0, NY - 1)], recv_sem.at[S_LY])
+    by_z[z] = ordered_sum(by_y, NY)
+    for d in Z_ORDER:
+        send(by_z.at[z], by_z.at[z], S_LZ, recv_sem.at[S_LZ], lax.rem(z + d, NZ) * NY + y, row)
+    pending.append((by_z.at[pl.ds(0, NZ - 1)], S_LZ))
     for g in range(GROUPS - 1):
         own_code_grad(g)
 
     wait(sums.at[pl.ds(0, ROWS - 1)], recv_sem.at[S_SUM])
-    summed = sums[0]
-    for r in range(1, ROWS):
-        summed = summed + sums[r]
+    summed = ordered_sum(sums, ROWS)
     benc = jnp.concatenate([summed[k : k + 1] for k in range(LAT // 128)], axis=1)
     high = benc.astype(BF16)
     middle = (benc - high.astype(F32)).astype(BF16)
@@ -286,24 +324,18 @@
     three = jnp.concatenate([high, middle, low, jnp.zeros((13, LAT), BF16)], axis=0)
     term = jnp.dot(three, wenc_t[...], preferred_element_type=F32)
     term = term[0:1] + (term[1:2] + term[2:3])
-    pieces = [
-        jnp.where(member // NY == k, ended_row, 0.0) - term[:, 128 * k : 128 * k + 128] for k in range(WIDTH // 128)
-    ]
-    by[y] = jnp.concatenate(pieces + [summed[6:7], jnp.zeros((3, 128), F32)], axis=0)
-    for d in Y_ORDER:
-        send(by.at[y], by.at[y], S_BY, recv_sem.at[S_BY], z * NY + lax.rem(y + d, NY), row)
-    pending.append((by.at[pl.ds(0, NY - 1)], S_BY))
+    bias = jnp.concatenate([jnp.where(own // NY == k, ended[...], 0.0) for k in range(2)], axis=1) - term
+    pieces = [bias[:, 128 * k : 128 * k + 128] for k in range(WIDTH // 128)]
+    biases[lat, 0:4] = jnp.concatenate(pieces, axis=0)
+    for dz, dy in L_ORDER:
+        to = lax.rem(z + dz, NZ) * NY + lax.rem(y + dy, NY)
+        mine = biases.at[lat, pl.ds(0, 4)]
+        send(mine, mine, S_BIAS, recv_sem.at[S_BIAS], to, row)
+    pending.append((biases.at[pl.ds(0, NY * NZ - 1), pl.ds(0, 4)], S_BIAS))
     grad_benc[...] = benc
 
     own_code_grad(GROUPS - 1)
     pending.append((code_in.at[:, pl.ds(0, ROWS - 1)], S_PG))
-
-    wait(by.at[pl.ds(0, NY - 1)], recv_sem.at[S_BY])
-    bz[z] = (by[0] + by[1]) + (by[2] + by[3])
-    for d in Z_ORDER:
-        to = lax.rem(z + d, NZ)
-        send(bz.at[z], bz.at[z], S_BZ, recv_sem.at[S_BZ], to * NY + y, row)
-    pending.append((bz.at[pl.ds(0, NZ - 1)], S_BZ))
 
     wait(code_in.at[:, pl.ds(0, ROWS - 1)], recv_sem.at[S_PG])
     genc[...] = lax.dot_general(
@@ -312,27 +344,45 @@
     put_enc = pltpu.make_async_copy(genc, grad_enc, local_sem.at[L_GENC])
     put_enc.start()
 
+    @pl.when(is_owner)
+    def _():
+        wait(parts.at[:, pl.ds(0, OWNERS - 1)], send_sem.at[S_PART])
+        wait(far, send_sem.at[S_FAR])
+        wait(grads.at[:, pl.ds(0, MEMBERS - 1)], send_sem.at[S_GRAD])
+
+    @pl.when(jnp.logical_not(is_owner))
+    def _():
+        wait(parts.at[:, pl.ds(0, OWNERS)], send_sem.at[S_PART])
+
     for ref, sem in pending:
         wait(ref, send_sem.at[sem])
     put_dec.wait()
     put_enc.wait()
-    wait(bz.at[pl.ds(0, NZ - 1)], recv_sem.at[S_BZ])
-    everything = bz[0]
-    for p in range(1, NZ):
-        everything = everything + bz[p]
-    tail[...] = everything
-
-
-def finish(genc, benc, gdec, tail, grad_enc, grad_benc, grad_dec, grad_bdec, losses, sem):
-    put_enc = pltpu.make_async_copy(genc, grad_enc, sem.at[0])
-    put_dec = pltpu.make_async_copy(gdec, grad_dec, sem.at[1])
-    put_enc.start()
-    put_dec.start()
-    grad_benc[...] = benc[...].reshape(LAT)
-    grad_bdec[...] = tail[0:4].reshape(WIDTH)
-    losses[...] = (tail[4] * (1.0 / (B * WIDTH * ROWS)))[0:PREFIXES]
-    put_enc.wait()
-    put_dec.wait()
+    wait(by_z.at[pl.ds(0, NZ - 1)], recv_sem.at[S_LZ])
+    tail[4:5] = ordered_sum(by_z, NZ)
+    wait(biases.at[pl.ds(0, NY * NZ - 1), pl.ds(0, 4)], recv_sem.at[S_BIAS])
+    quarters = []
+    for first in range(0, NY * NZ, NZ):
+        quarter = biases[first, 0:4]
+        for i in range(first + 1, first + NZ):
+            quarter = quarter + biases[i, 0:4]
+        quarters.append(quarter)
+    tail[0:4] = (quarters[0] + quarters[1]) + (quarters[2] + quarters[3])
+
+
+def finish(genc, benc, gdec, tail, *refs):
+    (outs, flat, sem) = (refs[:5], refs[5:8], refs[8])
+    sources = (genc, flat[0], gdec, flat[1], flat[2])
+    puts = [pltpu.make_async_copy(sources[i], outs[i], sem.at[i]) for i in range(5)]
+    puts[0].start()
+    puts[2].start()
+    flat[0][...] = benc[...].reshape(LAT)
+    flat[1][...] = tail[0:4].reshape(WIDTH)
+    flat[2][...] = (tail[4] * (1.0 / (B * WIDTH * ROWS)))[0:PREFIXES]
+    for i in (1, 3, 4):
+        puts[i].start()
+    for put in puts:
+        put.wait()
 
 
 def per_device(store, batch_rows, bounds, w_enc, b_enc, w_dec, b_dec):
@@ -368,9 +418,12 @@
             pltpu.VMEM((GROUPS, RT, CB), F32),
             pltpu.VMEM((B, LAT), BF16),
             pltpu.VMEM((B, WIDTH), BF16),
-            pltpu.VMEM((GROUPS, MEMBERS, RT, 128), BF16),
-            pltpu.VMEM((GROUPS, CLUSTERS, 2, RT, 128), BF16),
-            pltpu.VMEM((GROUPS, MEMBERS, RT, 128), BF16),
+            pltpu.VMEM((GROUPS, MEMBERS, RT, HALF), BF16),
+            pltpu.VMEM((GROUPS, 2, RT, HALF), BF16),
+            pltpu.VMEM((GROUPS, CLUSTERS - 1, RT, HALF), BF16),
+            pltpu.VMEM((GROUPS, MEMBERS, RT, HALF), BF16),
+            pltpu.VMEM((1, 128), F32),
+            pltpu.VMEM((1, HALF), F32),
             pltpu.VMEM((B, WIDTH), BF16),
             pltpu.VMEM((B, LAT), BF16),
             pltpu.VMEM((GROUPS, ROWS, RT, CB), BF16),
@@ -378,11 +431,13 @@
             pltpu.VMEM((ROWS, 8, 128), F32),
             pltpu.VMEM((LAT, WIDTH), BF16),
             pltpu.VMEM((WIDTH, LAT), BF16),
-            pltpu.VMEM((NY, 8, 128), F32),
-            pltpu.VMEM((NZ, 8, 128), F32),
+            pltpu.VMEM((NY * NZ, 8, 128), F32),
+            pltpu.VMEM((ROWS, 1, 128), F32),
+            pltpu.VMEM((NY, 1, 128), F32),
+            pltpu.VMEM((NZ, 1, 128), F32),
             pltpu.SemaphoreType.DMA((9,)),
-            pltpu.SemaphoreType.DMA((23,)),
-            pltpu.SemaphoreType.DMA((23,)),
+            pltpu.SemaphoreType.DMA((25,)),
+            pltpu.SemaphoreType.DMA((25,)),
             pltpu.SemaphoreType.REGULAR((2,)),
         ],
         compiler_params=pltpu.CompilerParams(
@@ -400,8 +455,13 @@
             jax.ShapeDtypeStruct((PREFIXES,), F32),
         ),
         in_specs=[hbm, vmem, hbm, vmem],
-        out_specs=(hbm, vmem, hbm, vmem, vmem),
-        scratch_shapes=[pltpu.SemaphoreType.DMA((2,))],
+        out_specs=[hbm] * 5,
+        scratch_shapes=[
+            pltpu.VMEM((LAT,), F32),
+            pltpu.VMEM((WIDTH,), F32),
+            pltpu.VMEM((PREFIXES,), F32),
+            pltpu.SemaphoreType.DMA((5,)),
+        ],
         compiler_params=pltpu.CompilerParams(vmem_limit_bytes=40 * 2**20),
         name="sae_finish",
     )(genc, benc, gdec, tail)

time: 66 us -> 64.4 us (0.976)
  Pallas kernels: 65.3 us -> 63.6 us
    pallas_call x1, Pallas kernels: 63.5 us -> 62.4 us  [per_device(): pl.pallas_call(kernel, out_shape=(jax.ShapeDtypeStruct((WIDTH, LAT), BF16...]
where the time goes in v4:
time: 64.4 us; the launch traced here: 64.3 us
  Pallas kernels  63.6 us (99%)
    pallas_call x1, Pallas kernels, per_device(): pl.pallas_call(kernel, out_shape=(jax.ShapeDtypeStruct((WIDTH, LAT), BF16...  62.4 us

profile of v4, /device:TPU:1, one launch (start us, length us, event | category | flops | bytes accessed | tf_op | source)
XLA Modules:
  0.0 64.3 jit_solution(3082589387652205247)
XLA Ops:
  0.6 62.4 %sae_step.1 = (bf16[512,768]{1,0:T(8,128)(2,1)S(1)}, f32[1,768]{1,0:T(1,128)S(1)}, bf16[768,512]{1,0:T(8,128)(2,1)S(1)}, f32[8,128]{1,0:T(8,128)S(1)}) custom-call(bf16[48,4096]{1,0:T(8,128)(2,1)} %store.1, s32[1,192]{1,0:T(1,128)} %bitcast.3, s32[5]{0:T(128)} %bounds_hbm.1, bf16[512,768]{1,0:T(8,128)(2,1)} %w_enc.1, f32[768]{0:T(1024)} %b_enc_hbm.1, ...), custom_call_target="tpu_custom_call" | custom-call | tf_op jit(solution)/shard_map/sae_step/pallas_call | solution.py:391
  63.1 1.2 %sae_finish.1 = (bf16[512,768]{1,0:T(8,128)(2,1)}, f32[768]{0:T(1024)}, bf16[768,512]{1,0:T(8,128)(2,1)}, f32[512]{0:T(512)}, f32[5]{0:T(128)}) custom-call(bf16[512,768]{1,0:T(8,128)(2,1)S(1)} %get-tuple-element.9.genc, f32[1,768]{1,0:T(1,128)S(1)} %get-tuple-element.10.benc, bf16[768,512]{1,0:T(8,128)(2,1)S(1)} %get-tuple-element.11.gdec, ...), custom_call_target="tpu_custom_call" | custom-call | tf_op jit(solution)/shard_map/sae_finish/pallas_call | solution.py:448

commit v5 on v4

--- a/solution.py
+++ b/solution.py
@@ -27,9 +27,9 @@
     ((dz, dy) for dz in range(NZ) for dy in range(NY) if dz or dy),
     key=lambda d: -(min(d[0], NZ - d[0]) + min(d[1], NY - d[1])),
 )
-O_ORDER = (6, 2, 5, 7, 1, 3, 4, 0)
-
-L_ENC, L_DEC, L_STORE, L_GDEC, L_GENC, L_ROWS, L_BENC, L_BDEC, L_BOUNDS = range(9)
+O_ORDER = (2, 1, 3, 0, 6, 5, 7, 4)
+
+L_ENC, L_DEC, L_STORE, L_GDEC, L_GENC, L_ROWS, L_BENC, L_BDEC, L_BOUNDS, L_GBENC, L_TAIL = range(11)
 S_PRE, S_CODES, S_PART, S_FAR, S_GRAD, S_CODE = range(0, 18, 3)
 S_STORE, S_PG, S_SUM, S_BIAS, S_LROW, S_LY, S_LZ = range(18, 25)
 
@@ -42,9 +42,9 @@
 
 
 def kernel(
-    store, batch_rows_hbm, bounds_hbm, w_enc, b_enc_hbm, w_dec, b_dec_hbm,
-    grad_enc, grad_benc, grad_dec, tail,
-    batch_rows, bounds, b_enc_flat, b_enc, b_dec, wenc, wdec, wenc_t, wdec_t, slope, picks, cols, target, centred, pre_out, pre_in, sig, codes, part_out, parts, near, far,
+    store_hbm, batch_rows_hbm, bounds_hbm, w_enc, b_enc_hbm, w_dec, b_dec_hbm,
+    grad_enc, grad_benc_out, grad_dec, tail_out,
+    grad_benc, tail,    store, batch_rows, bounds, b_enc_flat, b_enc, b_dec, wenc, wdec, wenc_t, wdec_t, slope, picks, cols, target, centred, pre_out, pre_in, sig, codes, part_out, parts, near, far,
     grads, losses, ended, pgrad, code_out, code_in, pgb, sums, gdec, genc, biases, by_row, by_y, by_z,
     local_sem, send_sem, recv_sem, relay_sem,
 ):
@@ -82,9 +82,8 @@
 
     get_enc = pltpu.make_async_copy(w_enc, wenc, local_sem.at[L_ENC])
     get_dec = pltpu.make_async_copy(w_dec, wdec, local_sem.at[L_DEC])
-    own_cols = pl.ds(pl.multiple_of(row * WIDTH, WIDTH), WIDTH)
     own_slot = pl.ds(pl.multiple_of(row * SB, SB), SB)
-    get_own = pltpu.make_async_copy(store.at[:, own_cols], cols.at[own_slot], local_sem.at[L_STORE])
+    get_own = pltpu.make_async_copy(store_hbm, store, local_sem.at[L_STORE])
     get_rows = pltpu.make_async_copy(batch_rows_hbm, batch_rows, local_sem.at[L_ROWS])
     get_benc = pltpu.make_async_copy(b_enc_hbm, b_enc_flat, local_sem.at[L_BENC])
     get_bdec = pltpu.make_async_copy(b_dec_hbm, b_dec, local_sem.at[L_BDEC])
@@ -116,12 +115,14 @@
 
     pass_on()
 
+    get_own.wait()
     for xx, cc in row_peers():
         to = xx * NC + cc
         their_cols = pl.ds(pl.multiple_of(to * WIDTH, WIDTH), WIDTH)
         send(store.at[:, their_cols], cols.at[own_slot], S_STORE, recv_sem.at[S_STORE], lat, to)
     pending.append((cols.at[pl.ds(0, SB * (ROWS - 1))], S_STORE))
-    for get in gets:
+    cols[own_slot] = store[:, pl.ds(pl.multiple_of(row * WIDTH, WIDTH), WIDTH)]
+    for get in gets[1:]:
         get.wait()
     b_enc[...] = b_enc_flat[...].reshape(1, LAT)
     rows_down = jnp.broadcast_to(batch_rows[...], (128, B)).T
@@ -155,16 +156,16 @@
         block(codes, g, x, c)[...] = (jnp.maximum(preact, 0.0) + log1p).astype(BF16)
         for xx, cc in row_peers():
             send(block(codes, g, x, c), block(codes, g, x, c), S_CODES, recv_sem.at[S_CODES + g], lat, xx * NC + cc)
+        if g < 2:
+            relay(last=g == 1)
         sig[g] = jnp.where(preact >= 0.0, 1.0, small) / (1.0 + small)
     pending.append((pre_in.at[:, pl.ds(0, ROWS - 1)], S_CODES))
 
-    relay()
-    relay(last=True)
     for g in range(GROUPS):
         wait(pre_in.at[g, pl.ds(0, ROWS - 1)], recv_sem.at[S_CODES + g])
         part_out[group(g)] = jnp.dot(codes[group(g)], wdec[...], preferred_element_type=F32).astype(BF16)
         for d in O_ORDER:
-            to = lax.rem(own + d, OWNERS)
+            to = lax.rem(lax.rem(member, NY) + d, NY) + NY * lax.rem(jnp.where(member < 2 * NY, 1, 0) + d // NY, 2)
 
             @pl.when(to + NY != member)
             def _():
@@ -228,12 +229,13 @@
             for j in range(MEMBERS - 1, -1, -1):
                 suffix = suffix + ends_at[j] * inclusive[j]
                 grads[g, j] = (-2.0 / B * suffix).astype(BF16)
-            for d in Z_ORDER:
-                to = lax.rem(member + d, MEMBERS)
-                send(
-                    grads.at[g, to], part(pgrad, g, own), S_GRAD, recv_sem.at[S_GRAD + g],
-                    cluster * MEMBERS + to, row,
-                )
+            for plane in (3, 0, 2, 1):
+                for d in (Y_ORDER if plane == 1 else Y_ORDER + (0,)):
+                    to = NY * jnp.where(member < 2 * NY, plane, 3 - plane) + lax.rem(member + d, NY)
+                    send(
+                        grads.at[g, to], part(pgrad, g, own), S_GRAD, recv_sem.at[S_GRAD + g],
+                        cluster * MEMBERS + to, row,
+                    )
             part(pgrad, g, own)[...] = grads[g, member]
             for k in range(PREFIXES):
                 error = ends[0][k] * inclusive[0]
@@ -270,7 +272,6 @@
             wait(grads.at[g, pl.ds(0, OWNERS)], recv_sem.at[S_GRAD + g])
 
         partial = jnp.dot(pgrad[group(g)], wdec_t[...], preferred_element_type=F32)
-        code_out[group(g)] = partial.astype(BF16)
         products = partial * slope[group(g)]
         for i in range(0, GR, 8):
             down = down + products[i : i + 8]
@@ -280,6 +281,7 @@
             sums[row] = jnp.concatenate(pieces + [jnp.zeros((2, 128), F32)], axis=0)
             for xx, cc in row_peers():
                 send(sums.at[row], sums.at[row], S_SUM, recv_sem.at[S_SUM], lat, xx * NC + cc)
+        code_out[group(g)] = partial.astype(BF16)
         for xx, cc in row_peers():
             send(block(code_out, g, xx, cc), code_in.at[g, row], S_CODE, recv_sem.at[S_CODE + g], lat, xx * NC + cc)
         code_in[g, row] = block(code_out, g, x, c)[...]
@@ -295,8 +297,6 @@
     gdec[...] = lax.dot_general(
         codes[...], pgrad[...], (((0,), (0,)), ((), ())), preferred_element_type=F32
     ).astype(BF16)
-    put_dec = pltpu.make_async_copy(gdec, grad_dec, local_sem.at[L_GDEC])
-    put_dec.start()
 
     def own_code_grad(g):
         wait(code_in.at[g, pl.ds(0, ROWS - 1)], recv_sem.at[S_CODE + g])
@@ -333,6 +333,10 @@
         send(mine, mine, S_BIAS, recv_sem.at[S_BIAS], to, row)
     pending.append((biases.at[pl.ds(0, NY * NZ - 1), pl.ds(0, 4)], S_BIAS))
     grad_benc[...] = benc
+    put_benc = pltpu.make_async_copy(grad_benc, grad_benc_out, local_sem.at[L_GBENC])
+    put_benc.start()
+    put_dec = pltpu.make_async_copy(gdec, grad_dec, local_sem.at[L_GDEC])
+    put_dec.start()
 
     own_code_grad(GROUPS - 1)
     pending.append((code_in.at[:, pl.ds(0, ROWS - 1)], S_PG))
@@ -359,7 +363,7 @@
     put_dec.wait()
     put_enc.wait()
     wait(by_z.at[pl.ds(0, NZ - 1)], recv_sem.at[S_LZ])
-    tail[4:5] = ordered_sum(by_z, NZ)
+    tail[4:8] = jnp.broadcast_to(ordered_sum(by_z, NZ), (4, 128))
     wait(biases.at[pl.ds(0, NY * NZ - 1), pl.ds(0, 4)], recv_sem.at[S_BIAS])
     quarters = []
     for first in range(0, NY * NZ, NZ):
@@ -368,6 +372,10 @@
             quarter = quarter + biases[i, 0:4]
         quarters.append(quarter)
     tail[0:4] = (quarters[0] + quarters[1]) + (quarters[2] + quarters[3])
+    put_tail = pltpu.make_async_copy(tail, tail_out, local_sem.at[L_TAIL])
+    put_tail.start()
+    put_benc.wait()
+    put_tail.wait()
 
 
 def finish(genc, benc, gdec, tail, *refs):
@@ -397,8 +405,11 @@
             jax.ShapeDtypeStruct((8, 128), F32),
         ),
         in_specs=[hbm] * 7,
-        out_specs=(hbm, vmem, hbm, vmem),
+        out_specs=[hbm] * 4,
         scratch_shapes=[
+            pltpu.VMEM((1, LAT), F32),
+            pltpu.VMEM((8, 128), F32),
+            pltpu.VMEM((SB, WIDTH * ROWS), BF16),
             pltpu.VMEM((1, B), jnp.int32),
             pltpu.SMEM((PREFIXES,), jnp.int32),
             pltpu.VMEM((LAT,), F32),
@@ -435,7 +446,7 @@
             pltpu.VMEM((ROWS, 1, 128), F32),
             pltpu.VMEM((NY, 1, 128), F32),
             pltpu.VMEM((NZ, 1, 128), F32),
-            pltpu.SemaphoreType.DMA((9,)),
+            pltpu.SemaphoreType.DMA((11,)),
             pltpu.SemaphoreType.DMA((25,)),
             pltpu.SemaphoreType.DMA((25,)),
             pltpu.SemaphoreType.REGULAR((2,)),

time: 64.4 us -> 63.1 us (0.980)
  Pallas kernels: 63.6 us -> 62.3 us
    pallas_call x1, Pallas kernels: 62.4 us -> 61.2 us  [per_device(): pl.pallas_call(kernel, out_shape=(jax.ShapeDtypeStruct((WIDTH, LAT), BF16...]
where the time goes in v5:
time: 63.1 us; the launch traced here: 63 us
  Pallas kernels  62.3 us (99%)
  between operations  0.64 us (1%)
    pallas_call x1, Pallas kernels, per_device(): pl.pallas_call(kernel, out_shape=(jax.ShapeDtypeStruct((WIDTH, LAT), BF16...  61.2 us

profile of v5, /device:TPU:1, one launch (start us, length us, event | category | flops | bytes accessed | tf_op | source)
XLA Modules:
  0.0 63.0 jit_solution(17269780631699462078)
XLA Ops:
  0.6 61.2 %sae_step.1 = (bf16[512,768]{1,0:T(8,128)(2,1)S(1)}, f32[1,768]{1,0:T(1,128)S(1)}, bf16[768,512]{1,0:T(8,128)(2,1)S(1)}, f32[8,128]{1,0:T(8,128)S(1)}) custom-call(bf16[48,4096]{1,0:T(8,128)(2,1)} %store_hbm.1, s32[1,192]{1,0:T(1,128)} %bitcast.3, s32[5]{0:T(128)} %bounds_hbm.1, bf16[512,768]{1,0:T(8,128)(2,1)} %w_enc.1, f32[768]{0:T(1024)} %b_enc_hbm.1, ...), custom_call_target="tpu_custom_call" | custom-call | tf_op jit(solution)/shard_map/sae_step/pallas_call | solution.py:399
  61.8 1.2 %sae_finish.1 = (bf16[512,768]{1,0:T(8,128)(2,1)}, f32[768]{0:T(1024)}, bf16[768,512]{1,0:T(8,128)(2,1)}, f32[512]{0:T(512)}, f32[5]{0:T(128)}) custom-call(bf16[512,768]{1,0:T(8,128)(2,1)S(1)} %get-tuple-element.9.genc, f32[1,768]{1,0:T(1,128)S(1)} %get-tuple-element.10.benc, bf16[768,512]{1,0:T(8,128)(2,1)S(1)} %get-tuple-element.11.gdec, ...), custom_call_target="tpu_custom_call" | custom-call | tf_op jit(solution)/shard_map/sae_finish/pallas_call | solution.py:459

commit v6 on v5

--- a/solution.py
+++ b/solution.py
@@ -20,7 +20,7 @@
 MEMBERS, CLUSTERS, OWNERS = 16, 4, 8
 HALF = WIDTH // 2
 
-X_ORDER = ((2, 0), (2, 1), (1, 0), (1, 1), (3, 0), (3, 1), (0, 1))
+X_ORDER = ((2, 0), (2, 1), (1, 0), (3, 0), (1, 1), (3, 1), (0, 1))
 Z_ORDER = (8, 7, 9, 6, 10, 5, 11, 4, 12, 3, 13, 2, 14, 1, 15)
 Y_ORDER = (2, 1, 3)
 L_ORDER = sorted(

time: 63.1 us -> 63.2 us (level)
  no operation moved by 1% of the time
where the time goes in v6:
time: 63.2 us; the launch traced here: 63.1 us
  Pallas kernels  62.5 us (99%)
  between operations  0.64 us (1%)
    pallas_call x1, Pallas kernels, per_device(): pl.pallas_call(kernel, out_shape=(jax.ShapeDtypeStruct((WIDTH, LAT), BF16...  61.3 us

profile of v6, /device:TPU:1, one launch (start us, length us, event | category | flops | bytes accessed | tf_op | source)
XLA Modules:
  0.0 63.1 jit_solution(266527098191190916)
XLA Ops:
  0.6 61.3 %sae_step.1 = (bf16[512,768]{1,0:T(8,128)(2,1)S(1)}, f32[1,768]{1,0:T(1,128)S(1)}, bf16[768,512]{1,0:T(8,128)(2,1)S(1)}, f32[8,128]{1,0:T(8,128)S(1)}) custom-call(bf16[48,4096]{1,0:T(8,128)(2,1)} %store_hbm.1, s32[1,192]{1,0:T(1,128)} %bitcast.3, s32[5]{0:T(128)} %bounds_hbm.1, bf16[512,768]{1,0:T(8,128)(2,1)} %w_enc.1, f32[768]{0:T(1024)} %b_enc_hbm.1, ...), custom_call_target="tpu_custom_call" | custom-call | tf_op jit(solution)/shard_map/sae_step/pallas_call | solution.py:399
  61.9 1.2 %sae_finish.1 = (bf16[512,768]{1,0:T(8,128)(2,1)}, f32[768]{0:T(1024)}, bf16[768,512]{1,0:T(8,128)(2,1)}, f32[512]{0:T(512)}, f32[5]{0:T(128)}) custom-call(bf16[512,768]{1,0:T(8,128)(2,1)S(1)} %get-tuple-element.9.genc, f32[1,768]{1,0:T(1,128)S(1)} %get-tuple-element.10.benc, bf16[768,512]{1,0:T(8,128)(2,1)S(1)} %get-tuple-element.11.gdec, ...), custom_call_target="tpu_custom_call" | custom-call | tf_op jit(solution)/shard_map/sae_finish/pallas_call | solution.py:459
